TPU v7x, 32 devices: a whole 2x2x4 slice. The times are simulated.
32 devices in a mesh: expert: 8 (over z, y), unit: 4 (over x, core).
Axes of the slice: x: 2, y: 2, z: 4, core: 2. Of those that a mesh axis runs over, the one named last changes fastest.
Arguments:
- w_up: bfloat16 [32, 1536, 4096], P('expert', 'unit'), may hold values from -0.09375 to 0.09375
- cluster: int32 [32, 1], replicated, may hold values from 0 to 7
- counts: int32 [32], replicated, may hold values from 16 to 127
Outputs:
- merged: bfloat16 [8, 1536, 4096], P('expert', None, 'unit')
Inputs may be any that keep to these rules, and one draw needn't show every extreme that they name: Every cluster has at least one member.
All inputs are finite; a program needn't handle non-finite values.
Results may differ from a plain program's by a relative error of at most 0.0051.
Values may be sent and summed in bfloat16 or wider, within the bound.
A program may use at most 128 MiB of HBM per device.

v0:
```python
import jax
import jax.numpy as jnp
from jax import lax
from jax.sharding import PartitionSpec as P

BLOCK = 96
NS_STEPS = 8
CLU_DEV = 1


def newton_schulz(matrices):
    frob_norm = jnp.sqrt(jnp.sum(matrices * matrices, axis=(-2, -1), keepdims=True) + 1e-06)
    value = matrices / frob_norm
    for iteration in range(NS_STEPS):
        square = jnp.einsum("...ij,...kj->...ik", value, value, precision=lax.Precision.HIGHEST)
        value = 1.5 * value - 0.5 * jnp.einsum(
            "...ik,...kj->...ij", square, value, precision=lax.Precision.HIGHEST
        )
    return value


def block_gram(left, right):
    experts, units, width = left.shape
    nblocks = units // BLOCK
    lead_rows = left.reshape(experts, nblocks, BLOCK, width)
    member_rows = right.reshape(experts, nblocks, BLOCK, width)
    gram = jnp.einsum("nbid,nbjd->nibj", lead_rows, member_rows, preferred_element_type=jnp.float32)
    return gram.reshape(experts, BLOCK, units)


def polar_factors(gram):
    experts, height, units = gram.shape
    nblocks = units // BLOCK
    matrices = gram.reshape(experts, BLOCK, nblocks, BLOCK).transpose(0, 2, 1, 3)
    polar = newton_schulz(matrices).astype(jnp.bfloat16)
    return polar.transpose(0, 2, 1, 3).reshape(experts, BLOCK, units)


def align_rows(factors, slab, scale):
    experts, units, width = slab.shape
    nblocks = units // BLOCK
    turn = factors.reshape(experts, BLOCK, nblocks, BLOCK)
    member_rows = slab.reshape(experts, nblocks, BLOCK, width)
    turned = jnp.einsum("nibj,nbjd->nbid", turn, member_rows, preferred_element_type=jnp.float32)
    turned = turned * scale[:, None, None, None]
    return turned.reshape(experts, units, width).astype(jnp.bfloat16)


def on_device(w_up, cluster, counts):
    cluster_ids = cluster[:, 0]
    experts = cluster_ids.shape[0]
    clusters = CLU_DEV * lax.axis_size("expert")
    index = jnp.arange(experts, dtype=jnp.int32)
    labels = jnp.arange(clusters, dtype=jnp.int32)
    member = cluster_ids[None, :] == labels[:, None]
    score = counts * experts + (experts - 1 - index)
    best = jnp.max(jnp.where(member, score[None, :], -1), axis=1)
    leader = experts - 1 - best % experts
    anchor_of = jnp.sum(jnp.where(member, leader[:, None], 0), axis=0)
    total = jnp.sum(jnp.where(member, counts[None, :], 0), axis=1).astype(jnp.float32)
    weight = counts.astype(jnp.float32) / jnp.sum(jnp.where(member, total[:, None], 0.0), axis=0)
    columns = lax.all_to_all(w_up, "expert", split_axis=2, concat_axis=0, tiled=True)
    anchors = jnp.take(columns, anchor_of, axis=0)
    gram = lax.psum_scatter(block_gram(anchors, columns), "expert", scatter_dimension=0, tiled=True)
    polar = polar_factors(gram)
    aligned = align_rows(lax.all_gather(polar, "expert", axis=0, tiled=True), columns, weight)
    select = member.astype(jnp.bfloat16)
    summed = jnp.dot(select, aligned.reshape(experts, -1), preferred_element_type=jnp.float32)
    merged = summed.reshape(clusters, aligned.shape[1], aligned.shape[2]).astype(jnp.bfloat16)
    return lax.all_to_all(
        lax.all_to_all(merged, "expert", split_axis=0, concat_axis=2, tiled=True),
        "unit",
        split_axis=2,
        concat_axis=1,
        tiled=True,
    )


def solution(mesh):
    return jax.shard_map(
        on_device,
        mesh=mesh,
        in_specs=(P("expert", "unit", None), P(), P()),
        out_specs=P("expert", None, "unit"),
        check_vma=False,
    )
```

profile of v0, /device:TPU:17, one launch (start us, length us, event | category | flops | bytes accessed | tf_op | source)
XLA Modules:
  0.0 780.7 jit_solution(14918757855871350126)
XLA Ops:
  6.5 20.1 %copy.32 = bf16[4,384,4096]{1,0,2:T(4,128)(2,1)} copy(bf16[4,384,4096]{2,1,0:T(8,128)(2,1)} %param.3) | data formatting | bytes 25165824 | tf_op args[0]
  26.7 0.0 copy-start
  26.7 0.0 copy-start.1
  26.7 5.7 all-to-all-start
  32.4 0.0 reduce-scatter.2.cloned.1.call-start
  32.4 0.0 copy-done
  32.4 0.0 copy-done.1
  32.4 0.1 select_reduce_fusion.3
  32.6 0.1 select_reduce_fusion.2
  32.7 268.8 %all-to-all-done = bf16[4,384,4096]{1,0,2:T(4,128)(2,1)} async-done(((bf16[4,384,4096]{1,0,2:T(4,128)(2,1)}), bf16[4,384,4096]{1,0,2:T(4,128)(2,1)}, u32[]{:S(2)}, u32[]{:S(2)}) %all-to-all-start) | async-done | bytes 12582944 | tf_op jit(solution)/shard_map/all_to_all | solution.py:62
  301.5 19.9 %copy.33 = bf16[4,384,8,512]{3,1,0,2:T(8,128)(2,1)} copy(bf16[4,384,8,512]{1,0,3,2:T(4,128)(2,1)} %bitcast.2) | data formatting | bytes 25165824 | tf_op jit(solution)/shard_map/all_to_all | solution.py:62
  321.3 11.2 %gather_fusion = bf16[32,384,512]{2,1,0:T(8,128)(2,1)} fusion(bf16[32,384,512]{2,1,0:T(8,128)(2,1)} %bitcast.121, s32[1024]{0:T(1024)S(1)} %pad_clamp_fusion), kind=kCustom, calls=%fused_computation | custom fusion | bytes 25165952 | tf_op jit(solution)/shard_map/jit(_take)/gather | solution.py:63
  332.6 10.1 %fusion.8 = f32[32,96,4,96]{3,1,2,0:T(8,128)S(1)} fusion(bf16[32,4,96,512]{3,2,1,0:T(8,128)(2,1)} %bitcast.122, bf16[32,4,96,512]{3,2,1,0:T(8,128)(2,1)} %bitcast.129, pred[32]{0:T(512)(128)(4,1)S(1)} %compare_and_fusion), kind=kOutput, calls=%fused_computation.10 | convolution fusion | flops 1214251008 | bytes 29884448 | tf_op jit(solution)/shard_map/nbid,nbjd->nibj/dot_general | solution.py:27
  342.6 7.9 %copy.34 = f32[32,96,4,96]{3,2,1,0:T(4,128)} copy(f32[32,96,4,96]{3,1,2,0:T(8,128)S(1)} %fusion.8) | data formatting | bytes 9437184 | tf_op jit(solution)/shard_map/nbid,nbjd->nibj/transpose | solution.py:27
  350.6 7.6 reshape.71
  358.2 0.0 reduce-scatter.2.cloned.1.call-update
  358.2 0.5 all-gather.2.cloned.1.call-start
  358.8 97.8 %reduce-scatter.2.cloned.1.call-done = f32[4,96,384]{2,1,0:T(8,128)} async-done(((f32[32,96,384]{2,1,0:T(8,128)}), f32[4,96,384]{2,1,0:T(8,128)}) %reduce-scatter.2.cloned.1.call-update) | async-done | bytes 589840 | tf_op jit(solution)/shard_map/reduce_scatter | solution.py:64
  456.6 1.5 reshape.72
  458.1 0.3 multiply_reduce_fusion
  458.5 1.8 fusion.25
  460.3 1.0 fusion.27
  461.3 1.7 fusion.43
  463.1 0.9 convolution_multiply_fusion.6
  464.0 1.8 fusion.41
  465.8 1.1 multiply_subtract_fusion.4
  466.9 1.8 fusion.44
  468.6 1.0 convolution_multiply_fusion.4
  469.6 1.8 fusion.42
  471.4 1.1 multiply_subtract_fusion.2
  472.5 1.9 fusion.45
  474.4 0.9 convolution_multiply_fusion.2
  475.3 1.7 fusion.40
  477.1 0.9 convolution_multiply_fusion.1
  478.0 1.9 fusion.28
  479.9 1.5 fusion.16
  481.4 0.2 copy.36
  481.6 1.0 reshape.73
  482.6 0.0 all-gather.2.cloned.1.call-update
  482.6 0.1 select_reduce_fusion
  482.7 50.8 %all-gather.2.cloned.1.call-done = bf16[32,96,384]{2,1,0:T(8,128)(2,1)} async-done(((bf16[4,96,384]{2,1,0:T(8,128)(2,1)}), bf16[32,96,384]{2,1,0:T(8,128)(2,1)}) %all-gather.2.cloned.1.call-update) | async-done | bytes 2359312 | tf_op jit(solution)/shard_map/all_gather | solution.py:66
  533.5 6.0 reshape.74
  539.5 12.5 %multiply_convert_fusion = bf16[32,4,96,512]{3,2,1,0:T(8,128)(2,1)} fusion(f32[32]{0:T(128)S(1)} %convert_divide_fusion, bf16[32,4,96,512]{3,2,1,0:T(8,128)(2,1)} %bitcast.123, bf16[32,96,4,96]{3,2,1,0:T(4,128)(2,1)S(1)} %reshape.74), kind=kOutput, calls=%fused_computation.1 | convolution fusion | flops 1220542464 | bytes 27525248 | tf_op jit(solution)/shard_map/nibj,nbjd->nbid/dot_general | solution.py:44
  552.0 12.7 %fusion.11 = bf16[8,384,512]{2,0,1:T(8,128)(2,1)S(1)} fusion(s32[32]{0:T(128)S(1)} %bitcast.133, bf16[4,8,384,512]{3,2,1,0:T(8,128)(2,1)} %bitcast.124), kind=kOutput, calls=%fused_computation.11 | convolution fusion | flops 102236416 | bytes 15728768 | tf_op jit(solution)/shard_map/dot_general | solution.py:68
  564.7 1.1 copy.39
  565.8 72.8 %all_to_all.54 = bf16[8,384,512]{2,1,0:T(8,128)(2,1)S(1)} all-to-all(bf16[8,384,512]{2,1,0:T(8,128)(2,1)S(1)} %copy.39), channel_id=1, replica_groups=mesh['expert'=8,'unit'=4] {'expert'}, dimensions={0} | all-to-all | bytes 6291456 | tf_op jit(solution)/shard_map/all_to_all | solution.py:71
  638.6 2.8 copy.40
  641.4 6.9 copy.71
  648.3 0.5 broadcast.147
  648.8 68.5 %reduce.1 = bf16[4096,384]{1,0:T(8,128)(2,1)} reduce(bf16[4096,1,384]{2,1,0:T(2,128)(2,1)} %bitcast.125, bf16[]{:T(256)} %broadcast.147), dimensions={1}, to_apply=%bitcast.120.reduce_sub_computation | reduce | bytes 6291458
  717.3 3.0 reshape.84
  720.3 40.8 %all_to_all.55 = bf16[4,2,196608]{2,1,0:T(2,128)(2,1)} all-to-all(bf16[4,2,196608]{2,1,0:T(2,128)(2,1)S(1)} %reshape.84), channel_id=1, replica_groups=mesh['expert'=8,'unit'=4] {'unit'}, dimensions={0} | all-to-all | bytes 6291456 | tf_op jit(solution)/shard_map/all_to_all | solution.py:70
  761.1 6.2 reshape.85
  767.3 3.3 copy.43
  770.6 2.9 copy.42
  (8 shorter events, 0.1 us)
Async XLA Ops:
  26.7 5.7 copy-start
  26.7 5.8 copy-start.1
  26.7 274.8 %all-to-all-start = ((bf16[4,384,4096]{1,0,2:T(4,128)(2,1)}), bf16[4,384,4096]{1,0,2:T(4,128)(2,1)}, u32[]{:S(2)}, u32[]{:S(2)}) async-start(bf16[4,384,4096]{1,0,2:T(4,128)(2,1)} %copy.32), calls=%async_computation | async-start | bytes 25165824 | tf_op jit(solution)/shard_map/all_to_all | solution.py:62
  32.4 424.2 %reduce-scatter.2.cloned.1.call-start = ((), (), s32[]{:S(2)}) async-start(), calls=%async_computation.4 | async-start | bytes 5308416 | tf_op jit(solution)/shard_map/reduce_scatter | solution.py:64
  358.2 175.3 %all-gather.2.cloned.1.call-start = ((), (), s32[]{:S(2)}) async-start(), calls=%async_computation.5 | async-start | bytes 2654208 | tf_op jit(solution)/shard_map/all_gather | solution.py:66
Sparse Core Ops, SparseCore 0:
  358.4 98.1 reduce-scatter.1
  482.7 50.7 all-gather.1
where the time goes:
time: 793 us; the launch traced here: 781 us
  waiting for transfers between devices  417 us (53%)
  blocking collectives  114 us (14%)
  local copies, waits for them, and re-layouts  102 us (13%)
  other arithmetic  69.2 us (9%)
  matrix products  58.1 us (7%)
  between operations  14.1 us (2%)
    all_to_all x1, waiting for transfers between devices, on_device(): lax.all_to_all(w_up, 'expert', split_axis=2, concat_axis=0, tiled=True)  269 us
    reduce_scatter x1, waiting for transfers between devices, on_device(): lax.psum_scatter(block_gram(anchors, columns), 'expert', scatter_dimensio...  97.8 us
    all_to_all x1, blocking collectives, on_device(): lax.all_to_all(merged, 'expert', split_axis=0, concat_axis=2, tiled=True)  72.8 us
    unnamed x1, other arithmetic  68.5 us
    all_gather x1, waiting for transfers between devices, on_device(): lax.all_gather(polar, 'expert', axis=0, tiled=True)  50.8 us
    all_to_all x1, blocking collectives, on_device(): lax.all_to_all(lax.all_to_all(merged, 'expert', split_axis=0, concat_axis...  40.8 us
    unnamed x9, local copies, waits for them, and re-layouts  33.1 us
    all_to_all x1, local copies, waits for them, and re-layouts, on_device(): lax.all_to_all(w_up, 'expert', split_axis=2, concat_axis=0, tiled=True)  19.9 us
  transfers between devices with their start and end apart: 3, of which 3 were waited for; matrix products, arithmetic and copies ran while one was open for 0% of the time, Pallas kernels for 0%

commit v1 on v0

v1 whole, which is shorter than its diff:
```python
import functools

import jax
import jax.numpy as jnp
from jax import lax
from jax.experimental import pallas as pl
from jax.experimental.pallas import tpu as pltpu
from jax.sharding import PartitionSpec as P

BLOCK = 96
NS_STEPS = 8
MESH = pl.DeviceIdType.MESH
VMEM_BYTES = 48 * 1024 * 1024


def newton_schulz(matrices):
    frob_norm = jnp.sqrt(jnp.sum(matrices * matrices, axis=(-2, -1), keepdims=True) + 1e-06)
    value = matrices / frob_norm
    for iteration in range(NS_STEPS):
        square = jnp.einsum("...ij,...kj->...ik", value, value, precision=lax.Precision.HIGH)
        value = 1.5 * value - 0.5 * jnp.einsum(
            "...ik,...kj->...ij", square, value, precision=lax.Precision.HIGH
        )
    return value


def deal_kernel(n, g, w_ref, slab_ref, local_sem, send_sem, recv_sem):
    me, unit = lax.axis_index("expert"), lax.axis_index("unit")
    cw = slab_ref.shape[-1]
    barrier = pltpu.get_barrier_semaphore()
    for d in range(1, n):
        pl.semaphore_signal(barrier, inc=1, device_id=(lax.rem(me + d, n), unit), device_id_type=MESH)
    pl.semaphore_wait(barrier, n - 1)

    def piece(peer):
        rows = pl.ds(pl.multiple_of((peer // g) * BLOCK, BLOCK), BLOCK)
        columns = pl.ds(pl.multiple_of(lax.rem(peer, g) * cw, cw), cw)
        return w_ref.at[:, rows, columns]

    copies = []
    for d in sorted(range(1, n), key=lambda d: abs(2 * d - n)):
        peer = lax.rem(me + d, n)
        copy = pltpu.make_async_remote_copy(
            src_ref=piece(peer),
            dst_ref=slab_ref.at[me],
            send_sem=send_sem.at[d],
            recv_sem=recv_sem.at[d],
            device_id=(peer, unit),
            device_id_type=MESH,
        )
        copy.start()
        copies.append(copy)
    own = pltpu.make_async_copy(piece(me), slab_ref.at[me], local_sem)
    own.start()
    own.wait()
    for copy in copies:
        copy.wait()


def deal(w, n, g):
    held, units, width = w.shape
    return pl.pallas_call(
        functools.partial(deal_kernel, n, g),
        out_shape=jax.ShapeDtypeStruct((n, held, BLOCK, width // g), w.dtype),
        in_specs=[pl.BlockSpec(memory_space=pl.ANY)],
        out_specs=pl.BlockSpec(memory_space=pl.ANY),
        scratch_shapes=[
            pltpu.SemaphoreType.DMA,
            pltpu.SemaphoreType.DMA((n,)),
            pltpu.SemaphoreType.DMA((n,)),
        ],
        compiler_params=pltpu.CompilerParams(
            collective_id=0, has_side_effects=True, vmem_limit_bytes=VMEM_BYTES
        ),
        cost_estimate=pl.CostEstimate(flops=0, bytes_accessed=4 * w.size, transcendentals=0),
        name="deal",
    )(w)


def gram_kernel(order_ref, anchor_ref, lead_ref, rows_ref, gram_ref):
    gram_ref[0] = lax.dot_general(
        lead_ref[0], rows_ref[0], (((1,), (1,)), ((), ())), preferred_element_type=jnp.float32
    )


def block_gram(order, anchor_of, slab):
    experts, _, cw = slab.shape
    return pl.pallas_call(
        gram_kernel,
        grid_spec=pltpu.PrefetchScalarGridSpec(
            num_scalar_prefetch=2,
            grid=(experts,),
            in_specs=[
                pl.BlockSpec((1, BLOCK, cw), lambda s, order, anchor: (anchor[order[s]], 0, 0)),
                pl.BlockSpec((1, BLOCK, cw), lambda s, order, anchor: (order[s], 0, 0)),
            ],
            out_specs=pl.BlockSpec((1, BLOCK, BLOCK), lambda s, order, anchor: (order[s], 0, 0)),
        ),
        out_shape=jax.ShapeDtypeStruct((experts, BLOCK, BLOCK), jnp.float32),
        compiler_params=pltpu.CompilerParams(vmem_limit_bytes=VMEM_BYTES),
        cost_estimate=pl.CostEstimate(
            flops=2 * slab.size * BLOCK, bytes_accessed=4 * slab.size, transcendentals=0
        ),
        name="gram",
    )(order, anchor_of, slab, slab)


def merge_kernel(order_ref, cluster_ref, weight_ref, factor_ref, rows_ref, merged_ref, total_ref):
    step = pl.program_id(0)
    expert = order_ref[step]
    last = order_ref[jnp.maximum(step - 1, 0)]
    opens = (step == 0) | (cluster_ref[last] != cluster_ref[expert])
    turned = jnp.dot(factor_ref[0], rows_ref[0], preferred_element_type=jnp.float32)
    aligned = (turned * weight_ref[expert]).astype(jnp.bfloat16).astype(jnp.float32)

    @pl.when(opens)
    def _():
        total_ref[...] = aligned

    @pl.when(jnp.logical_not(opens))
    def _():
        total_ref[...] += aligned

    merged_ref[0] = total_ref[...].astype(merged_ref.dtype)


def merge_rows(order, cluster_ids, weight, factors, slab, clusters):
    experts, _, cw = slab.shape
    return pl.pallas_call(
        merge_kernel,
        grid_spec=pltpu.PrefetchScalarGridSpec(
            num_scalar_prefetch=3,
            grid=(experts,),
            in_specs=[
                pl.BlockSpec((1, BLOCK, BLOCK), lambda s, order, ids, weight: (order[s], 0, 0)),
                pl.BlockSpec((1, BLOCK, cw), lambda s, order, ids, weight: (order[s], 0, 0)),
            ],
            out_specs=pl.BlockSpec((1, BLOCK, cw), lambda s, order, ids, weight: (ids[order[s]], 0, 0)),
            scratch_shapes=[pltpu.VMEM((BLOCK, cw), jnp.float32)],
        ),
        out_shape=jax.ShapeDtypeStruct((clusters, BLOCK, cw), slab.dtype),
        compiler_params=pltpu.CompilerParams(vmem_limit_bytes=VMEM_BYTES),
        cost_estimate=pl.CostEstimate(
            flops=2 * slab.size * BLOCK, bytes_accessed=3 * slab.size, transcendentals=0
        ),
        name="merge",
    )(order, cluster_ids, weight, factors, slab)


def serve_kernel(n, m, g, units, merged_ref, out_ref, local_sem, send_sem, recv_sem):
    me, unit = lax.axis_index("expert"), lax.axis_index("unit")
    cw, uw = merged_ref.shape[-1], out_ref.shape[-1]
    pw = min(cw, uw)
    parts = cw // pw

    def target(part):
        column = lax.rem(me, g) * cw + part * pw
        return column // uw, pl.multiple_of(lax.rem(column, uw), pw)

    def feeds(source):
        column = lax.rem(source, g) * cw
        return (column // uw <= unit) & (unit <= (column + cw - pw) // uw)

    barrier = pltpu.get_barrier_semaphore()
    for d in range(n):
        source = lax.rem(me + n - d, n)
        for u in range(m):
            @pl.when(feeds(source) & ((u != unit) | (d != 0)))
            def _():
                pl.semaphore_signal(barrier, inc=1, device_id=(source, u), device_id_type=MESH)
    own = feeds(me)
    pl.semaphore_wait(barrier, n * parts - own.astype(jnp.int32))

    rows = pl.ds(pl.multiple_of(unit * units + (me // g) * BLOCK, BLOCK), BLOCK)

    def remote(d, part):
        peer = lax.rem(me + d, n)
        to, offset = target(part)
        return pltpu.make_async_remote_copy(
            src_ref=merged_ref.at[peer, :, pl.ds(part * pw, pw)],
            dst_ref=out_ref.at[0, rows, pl.ds(offset, pw)],
            send_sem=send_sem.at[d, part],
            recv_sem=recv_sem.at[d, unit],
            device_id=(peer, to),
            device_id_type=MESH,
        )

    def local(part):
        _, offset = target(part)
        return pltpu.make_async_copy(
            merged_ref.at[me, :, pl.ds(part * pw, pw)], out_ref.at[0, rows, pl.ds(offset, pw)], local_sem
        )

    for d in sorted(range(n), key=lambda d: abs(2 * d - n)):
        for part in range(parts):
            if d:
                remote(d, part).start()
            else:
                mine = target(part)[0] == unit

                @pl.when(mine)
                def _():
                    local(part).start()

                @pl.when(jnp.logical_not(mine))
                def _():
                    remote(0, part).start()

    for d in range(n):
        for part in range(parts):
            if d:
                remote(d, part).wait_send()
            else:
                mine = target(part)[0] == unit

                @pl.when(mine)
                def _():
                    local(part).wait()

                @pl.when(jnp.logical_not(mine))
                def _():
                    remote(0, part).wait_send()

    for d in range(n):
        source = lax.rem(me + n - d, n)
        for u in range(m):
            @pl.when(feeds(source) & ((u != unit) | (d != 0)))
            def _():
                there = pl.ds(pl.multiple_of(u * units + (source // g) * BLOCK, BLOCK), BLOCK)
                column = pl.multiple_of(lax.rem(lax.rem(source, g) * cw, uw), pw)
                landed = out_ref.at[0, there, pl.ds(column, pw)]
                pltpu.make_async_remote_copy(
                    src_ref=landed,
                    dst_ref=landed,
                    send_sem=send_sem.at[0, 0],
                    recv_sem=recv_sem.at[d, u],
                    device_id=(source, u),
                    device_id_type=MESH,
                ).wait_recv()


def serve(merged, n, m, g, units, width):
    parts = max(1, merged.shape[-1] * m // width)
    return pl.pallas_call(
        functools.partial(serve_kernel, n, m, g, units),
        out_shape=jax.ShapeDtypeStruct((1, m * units, width // m), merged.dtype),
        in_specs=[pl.BlockSpec(memory_space=pl.ANY)],
        out_specs=pl.BlockSpec(memory_space=pl.ANY),
        scratch_shapes=[
            pltpu.SemaphoreType.DMA,
            pltpu.SemaphoreType.DMA((n, parts)),
            pltpu.SemaphoreType.DMA((n, m)),
        ],
        compiler_params=pltpu.CompilerParams(
            collective_id=1, has_side_effects=True, vmem_limit_bytes=VMEM_BYTES
        ),
        cost_estimate=pl.CostEstimate(flops=0, bytes_accessed=4 * merged.size, transcendentals=0),
        name="serve",
    )(merged)


def on_device(w_up, cluster, counts):
    n, m = lax.axis_size("expert"), lax.axis_size("unit")
    held, units, width = w_up.shape
    nblocks = units // BLOCK
    g = n // nblocks
    cluster_ids = cluster[:, 0]
    experts = cluster_ids.shape[0]
    index = jnp.arange(experts, dtype=jnp.int32)
    labels = jnp.arange(n, dtype=jnp.int32)
    member = cluster_ids[None, :] == labels[:, None]
    score = counts * experts + (experts - 1 - index)
    best = jnp.max(jnp.where(member, score[None, :], -1), axis=1)
    leader = experts - 1 - best % experts
    anchor_of = jnp.sum(jnp.where(member, leader[:, None], 0), axis=0)
    total = jnp.sum(jnp.where(member, counts[None, :], 0), axis=1).astype(jnp.float32)
    weight = counts.astype(jnp.float32) / jnp.sum(jnp.where(member, total[:, None], 0.0), axis=0)

    slab = deal(w_up, n, g).reshape(experts, BLOCK, width // g)
    before = (cluster_ids[None, :] < cluster_ids[:, None]) | (
        (cluster_ids[None, :] == cluster_ids[:, None]) & (index[None, :] < index[:, None])
    )
    place = jnp.sum(before.astype(jnp.int32), axis=1)
    order = jnp.sum(jnp.where(place[None, :] == index[:, None], index[None, :], 0), axis=1)
    partial = block_gram(order, anchor_of, slab)

    share = experts // g
    part = lax.axis_index("expert") % g

    def pairs(d):
        return [(e, e // g * g + (e + d) % g) for e in range(n)]

    gram = lax.dynamic_slice_in_dim(partial, part * share, share)
    for d in range(1, g):
        other = lax.dynamic_slice_in_dim(partial, (part + d) % g * share, share)
        gram = gram + lax.ppermute(other, "expert", pairs(d))
    polar = newton_schulz(gram).astype(jnp.bfloat16)
    factors = jnp.zeros((experts, BLOCK, BLOCK), jnp.bfloat16)
    factors = lax.dynamic_update_slice_in_dim(factors, polar, part * share, 0)
    for d in range(1, g):
        other = lax.ppermute(polar, "expert", pairs(d))
        factors = lax.dynamic_update_slice_in_dim(factors, other, (part + g - d) % g * share, 0)

    merged = merge_rows(order, cluster_ids, weight, factors, slab, n)
    return serve(merged, n, m, g, units, width)


def solution(mesh):
    return jax.shard_map(
        on_device,
        mesh=mesh,
        in_specs=(P("expert", "unit", None), P(), P()),
        out_specs=P("expert", None, "unit"),
        check_vma=False,
    )
```

time: 793 us -> 473 us (0.60); the launches traced: 781 us -> 471 us
  Pallas kernels: 0 us -> 426 us
  waiting for transfers between devices: 417 us -> 25.5 us
  blocking collectives: 114 us -> 0 us
  local copies, waits for them, and re-layouts: 102 us -> 3.56 us
  other arithmetic: 69.2 us -> 3.69 us
  matrix products: 58.1 us -> 12.2 us
  between operations: 14.1 us -> 0.24 us
    pallas_call x0 -> x4, Pallas kernels: none -> 426 us  [the longest x1 274 us: deal(): pl.pallas_call(functools.partial(deal_kernel, n, g), out_shape=jax.ShapeD...]
    all_to_all x1 -> x0, waiting for transfers between devices: 269 us -> none  [on_device(): lax.all_to_all(w_up, 'expert', split_axis=2, concat_axis=0, tiled=True)]
    all_to_all x2 -> x0, blocking collectives: 114 us -> none  [the longest x1 72.8 us: on_device(): lax.all_to_all(merged, 'expert', split_axis=0, concat_axis=2, tiled=True)]
    reduce_scatter x1 -> x0, waiting for transfers between devices: 97.8 us -> none  [on_device(): lax.psum_scatter(block_gram(anchors, columns), 'expert', scatter_dimensio...]
    unnamed x1 -> x0, other arithmetic: 68.5 us -> none
    all_gather x1 -> x0, waiting for transfers between devices: 50.8 us -> none  [on_device(): lax.all_gather(polar, 'expert', axis=0, tiled=True)]
    dot_general x11 -> x8, matrix products: 49.6 us -> 7.51 us  [newton_schulz(): jnp.einsum('...ij,...kj->...ik', value, value, precision=lax.Precision.HIGH)]
    all_to_all x4 -> x0, local copies, waits for them, and re-layouts: 32.4 us -> none  [the longest x1 19.9 us: on_device(): lax.all_to_all(w_up, 'expert', split_axis=2, concat_axis=0, tiled=True)]
  transfers between devices with their start and end apart: 3 -> 2, of which waited for: 3 -> 2; matrix products, arithmetic and copies ran while one was open for 0% -> 0% of each run, Pallas kernels for 0% -> 0%
where the time goes in v1:
time: 473 us; the launch traced here: 471 us
  Pallas kernels  426 us (90%)
  waiting for transfers between devices  25.5 us (5%)
  matrix products  12.2 us (3%)
    pallas_call x1, Pallas kernels, deal(): pl.pallas_call(functools.partial(deal_kernel, n, g), out_shape=jax.ShapeD...  274 us
    pallas_call x1, Pallas kernels, serve(): pl.pallas_call(functools.partial(serve_kernel, n, m, g, units), out_shape...  106 us
    pallas_call x1, Pallas kernels, merge_rows(): pl.pallas_call(merge_kernel, grid_spec=pltpu.PrefetchScalarGridSpec(num_s...  23.2 us
    pallas_call x1, Pallas kernels, block_gram(): pl.pallas_call(gram_kernel, grid_spec=pltpu.PrefetchScalarGridSpec(num_sc...  22.4 us
    ppermute x1, waiting for transfers between devices, on_device(): gram = gram + lax.ppermute(other, 'expert', pairs(d))  17.6 us
  transfers between devices with their start and end apart: 2, of which 2 were waited for; matrix products, arithmetic and copies ran while one was open for 0% of the time, Pallas kernels for 0%

profile of v1, /device:TPU:17, one launch (start us, length us, event | category | flops | bytes accessed | tf_op | source)
XLA Modules:
  0.0 471.4 jit_solution(12844592219661324640)
XLA Ops:
  0.0 0.7 subtract_add_fusion
  0.7 0.9 convert_reduce_fusion
  1.6 0.8 select_reduce_fusion.2
  2.4 0.9 select_reduce_fusion.1
  3.2 0.1 select_reduce_fusion.order_ref
  3.3 273.9 %deal.1 = bf16[8,4,96,2048]{3,2,1,0:T(8,128)(2,1)} custom-call(bf16[4,384,4096]{2,1,0:T(8,128)(2,1)} %w_ref.1), custom_call_target="tpu_custom_call" | custom-call | bytes 25165824 | tf_op jit(solution)/shard_map/deal/pallas_call | solution.py:62
  277.2 22.4 %gram.1 = f32[32,96,96]{2,1,0:T(8,128)S(1)} custom-call(s32[32]{0:T(128)S(1)} %select_reduce_fusion.order_ref, s32[32]{0:T(128)S(1)} %get-tuple-element.5.anchor_ref, bf16[32,96,2048]{2,1,0:T(8,128)(2,1)} %bitcast.36, bf16[32,96,2048]{2,1,0:T(8,128)(2,1)} %bitcast.37), custom_call_target="tpu_custom_call" | custom-call | flops 1207959552 | bytes 25165824 | tf_op jit(solution)/shard_map/gram/pallas_call | solution.py:88
  299.6 0.1 constant_dynamic-slice_fusion
  299.7 0.1 collective-permute-start
  299.8 17.6 %collective-permute-done = f32[16,96,96]{2,1,0:T(8,128)S(1)} collective-permute-done((f32[16,96,96]{2,1,0:T(8,128)S(1)}, f32[16,96,96]{2,1,0:T(8,128)S(1)}, u32[]{:S(2)}, u32[]{:S(2)}) %collective-permute-start) | collective-permute-done | bytes 589856 | tf_op jit(solution)/shard_map/ppermute | solution.py:296
  317.4 0.3 multiply_reduce_fusion
  317.6 1.0 fusion.11
  318.7 0.8 multiply_subtract_fusion.1
  319.4 0.9 fusion.12
  320.4 0.6 multiply_subtract_fusion
  321.0 0.9 fusion.13
  321.9 0.5 fusion.5
  322.4 0.9 fusion.14
  323.4 0.5 fusion.4
  323.9 0.9 fusion.15
  324.8 0.5 fusion.3
  325.4 0.9 fusion.16
  326.3 0.5 fusion.2
  326.9 0.9 fusion.17
  327.8 0.6 fusion.1
  328.4 0.9 fusion.18
  329.3 0.0 copy-start.1
  329.3 0.0 copy-start.2
  329.3 0.1 broadcast_in_dim.71
  329.4 0.7 constant_dynamic-update-slice_fusion
  330.1 0.4 collective-permute-start.1
  330.5 0.0 copy-done.1
  330.5 0.1 select_reduce_fusion.3
  330.6 0.0 copy-done.2
  330.6 7.9 %collective-permute-done.1 = bf16[16,96,96]{2,1,0:T(8,128)(2,1)S(1)} collective-permute-done((bf16[16,96,96]{2,1,0:T(8,128)(2,1)S(1)}, bf16[16,96,96]{2,1,0:T(8,128)(2,1)S(1)}, u32[]{:S(2)}, u32[]{:S(2)}) %collective-permute-start.1) | collective-permute-done | bytes 294944 | tf_op jit(solution)/shard_map/ppermute | solution.py:301
  338.5 0.1 constant_dynamic-update-slice_fusion.1.factor_ref
  338.5 23.2 %merge.1.merged_ref = bf16[8,96,2048]{2,1,0:T(8,128)(2,1)S(1)} custom-call(s32[32]{0:T(128)S(1)} %select_reduce_fusion.order_ref, s32[32]{0:T(128)S(1)} %bitcast.35, f32[32]{0:T(128)S(1)} %convert_divide_fusion.weight_ref, bf16[32,96,96]{2,1,0:T(8,128)(2,1)S(1)} %constant_dynamic-update-slice_fusion.1.factor_ref, bf16[32,96,2048]{2,1,0:T(8,128)(2,1)} %bitcast.38), custom_call_target="tpu_custom_call" | custom-call | flops 1207959552 | bytes 18874368 | tf_op jit(solution)/shard_map/merge/pallas_call | solution.py:129
  361.7 0.0 copy-start
  361.7 1.7 copy-done
  363.4 106.3 %serve.1 = bf16[1,1536,1024]{2,1,0:T(8,128)(2,1)S(1)} custom-call(bf16[8,96,2048]{2,1,0:T(8,128)(2,1)} %copy-done), custom_call_target="tpu_custom_call" | custom-call | bytes 6291456 | tf_op jit(solution)/shard_map/serve/pallas_call | solution.py:244
  469.7 1.7 copy.7
  (4 shorter events, 0.0 us)
Async XLA Ops:
  299.7 17.7 %collective-permute-start = (f32[16,96,96]{2,1,0:T(8,128)S(1)}, f32[16,96,96]{2,1,0:T(8,128)S(1)}, u32[]{:S(2)}, u32[]{:S(2)}) collective-permute-start(f32[16,96,96]{2,1,0:T(8,128)S(1)} %constant_dynamic-slice_fusion), channel_id=1, source_target_pairs={{0,4},{4,0},{8,12},{12,8},{16,20},{20,16},{24,28},{28,24},{1,5},{5... | collective-permute-start | bytes 1769480 | tf_op jit(solution)/shard_map/ppermute | solution.py:296
  329.3 1.2 copy-start.1
  329.3 1.2 copy-start.2
  330.1 8.3 %collective-permute-start.1 = (bf16[16,96,96]{2,1,0:T(8,128)(2,1)S(1)}, bf16[16,96,96]{2,1,0:T(8,128)(2,1)S(1)}, u32[]{:S(2)}, u32[]{:S(2)}) collective-permute-start(bf16[16,96,96]{2,1,0:T(8,128)(2,1)S(1)} %get-tuple-element.8), channel_id=1, source_target_pairs={{0,4},{4,0},{8,12},{12,8},{16,20},{20,16},{24,28},{28,24},{1,5},{5... | collective-permute-start | bytes 884744 | tf_op jit(solution)/shard_map/ppermute | solution.py:301
  361.7 1.7 copy-start

commit v2 on v1

--- a/solution.py
+++ b/solution.py
@@ -24,7 +24,7 @@
     return value
 
 
-def deal_kernel(n, g, w_ref, slab_ref, local_sem, send_sem, recv_sem):
+def deal_kernel(n, g, w_ref, slab_ref, ready_ref, local_sem, send_sem, recv_sem):
     me, unit = lax.axis_index("expert"), lax.axis_index("unit")
     cw = slab_ref.shape[-1]
     barrier = pltpu.get_barrier_semaphore()
@@ -55,15 +55,19 @@
     own.wait()
     for copy in copies:
         copy.wait()
+    ready_ref[...] = jnp.zeros_like(ready_ref)
 
 
 def deal(w, n, g):
-    held, units, width = w.shape
+    held, _, width = w.shape
     return pl.pallas_call(
         functools.partial(deal_kernel, n, g),
-        out_shape=jax.ShapeDtypeStruct((n, held, BLOCK, width // g), w.dtype),
+        out_shape=[
+            jax.ShapeDtypeStruct((n, held, BLOCK, width // g), w.dtype),
+            jax.ShapeDtypeStruct((8, 128), jnp.int32),
+        ],
         in_specs=[pl.BlockSpec(memory_space=pl.ANY)],
-        out_specs=pl.BlockSpec(memory_space=pl.ANY),
+        out_specs=[pl.BlockSpec(memory_space=pl.ANY), pl.BlockSpec(memory_space=pltpu.VMEM)],
         scratch_shapes=[
             pltpu.SemaphoreType.DMA,
             pltpu.SemaphoreType.DMA((n,)),
@@ -147,7 +151,7 @@
     )(order, cluster_ids, weight, factors, slab)
 
 
-def serve_kernel(n, m, g, units, merged_ref, out_ref, local_sem, send_sem, recv_sem):
+def serve_kernel(n, m, g, units, merged_ref, out_ref, ready_ref, local_sem, send_sem, recv_sem):
     me, unit = lax.axis_index("expert"), lax.axis_index("unit")
     cw, uw = merged_ref.shape[-1], out_ref.shape[-1]
     pw = min(cw, uw)
@@ -237,33 +241,57 @@
                     device_id=(source, u),
                     device_id_type=MESH,
                 ).wait_recv()
-
-
-def serve(merged, n, m, g, units, width):
+    ready_ref[...] = jnp.zeros_like(ready_ref)
+
+
+def serve(merged, n, m, g, units, width, collective_id):
     parts = max(1, merged.shape[-1] * m // width)
     return pl.pallas_call(
         functools.partial(serve_kernel, n, m, g, units),
-        out_shape=jax.ShapeDtypeStruct((1, m * units, width // m), merged.dtype),
+        out_shape=[
+            jax.ShapeDtypeStruct((1, m * units, width // m), merged.dtype),
+            jax.ShapeDtypeStruct((8, 128), jnp.int32),
+        ],
         in_specs=[pl.BlockSpec(memory_space=pl.ANY)],
-        out_specs=pl.BlockSpec(memory_space=pl.ANY),
+        out_specs=[pl.BlockSpec(memory_space=pl.ANY), pl.BlockSpec(memory_space=pltpu.VMEM)],
         scratch_shapes=[
             pltpu.SemaphoreType.DMA,
             pltpu.SemaphoreType.DMA((n, parts)),
             pltpu.SemaphoreType.DMA((n, m)),
         ],
         compiler_params=pltpu.CompilerParams(
-            collective_id=1, has_side_effects=True, vmem_limit_bytes=VMEM_BYTES
+            collective_id=collective_id, has_side_effects=True, vmem_limit_bytes=VMEM_BYTES
         ),
         cost_estimate=pl.CostEstimate(flops=0, bytes_accessed=4 * merged.size, transcendentals=0),
         name="serve",
     )(merged)
 
 
+def merge_blocks(slab, order, anchor_of, cluster_ids, weight, n, g):
+    experts = slab.shape[0]
+    partial = block_gram(order, anchor_of, slab)
+    share = experts // g
+    part = lax.axis_index("expert") % g
+
+    def pairs(d):
+        return [(e, e // g * g + (e + d) % g) for e in range(n)]
+
+    gram = lax.dynamic_slice_in_dim(partial, part * share, share)
+    for d in range(1, g):
+        other = lax.dynamic_slice_in_dim(partial, (part + d) % g * share, share)
+        gram = gram + lax.ppermute(other, "expert", pairs(d))
+    polar = newton_schulz(gram).astype(jnp.bfloat16)
+    factors = jnp.zeros((experts, BLOCK, BLOCK), jnp.bfloat16)
+    factors = lax.dynamic_update_slice_in_dim(factors, polar, part * share, 0)
+    for d in range(1, g):
+        other = lax.ppermute(polar, "expert", pairs(d))
+        factors = lax.dynamic_update_slice_in_dim(factors, other, (part + g - d) % g * share, 0)
+    return merge_rows(order, cluster_ids, weight, factors, slab, n)
+
+
 def on_device(w_up, cluster, counts):
     n, m = lax.axis_size("expert"), lax.axis_size("unit")
     held, units, width = w_up.shape
-    nblocks = units // BLOCK
-    g = n // nblocks
     cluster_ids = cluster[:, 0]
     experts = cluster_ids.shape[0]
     index = jnp.arange(experts, dtype=jnp.int32)
@@ -275,34 +303,40 @@
     anchor_of = jnp.sum(jnp.where(member, leader[:, None], 0), axis=0)
     total = jnp.sum(jnp.where(member, counts[None, :], 0), axis=1).astype(jnp.float32)
     weight = counts.astype(jnp.float32) / jnp.sum(jnp.where(member, total[:, None], 0.0), axis=0)
-
-    slab = deal(w_up, n, g).reshape(experts, BLOCK, width // g)
     before = (cluster_ids[None, :] < cluster_ids[:, None]) | (
         (cluster_ids[None, :] == cluster_ids[:, None]) & (index[None, :] < index[:, None])
     )
     place = jnp.sum(before.astype(jnp.int32), axis=1)
     order = jnp.sum(jnp.where(place[None, :] == index[:, None], index[None, :], 0), axis=1)
-    partial = block_gram(order, anchor_of, slab)
-
-    share = experts // g
-    part = lax.axis_index("expert") % g
-
-    def pairs(d):
-        return [(e, e // g * g + (e + d) % g) for e in range(n)]
-
-    gram = lax.dynamic_slice_in_dim(partial, part * share, share)
-    for d in range(1, g):
-        other = lax.dynamic_slice_in_dim(partial, (part + d) % g * share, share)
-        gram = gram + lax.ppermute(other, "expert", pairs(d))
-    polar = newton_schulz(gram).astype(jnp.bfloat16)
-    factors = jnp.zeros((experts, BLOCK, BLOCK), jnp.bfloat16)
-    factors = lax.dynamic_update_slice_in_dim(factors, polar, part * share, 0)
-    for d in range(1, g):
-        other = lax.ppermute(polar, "expert", pairs(d))
-        factors = lax.dynamic_update_slice_in_dim(factors, other, (part + g - d) % g * share, 0)
-
-    merged = merge_rows(order, cluster_ids, weight, factors, slab, n)
-    return serve(merged, n, m, g, units, width)
+
+    half = units // 2
+    g = n // (half // BLOCK)
+    cw = width // g
+    me = lax.axis_index("expert")
+    slab, ready = deal(w_up, n, g)
+    start = half + ready[0, 0]
+
+    def piece(peer):
+        return lax.dynamic_slice(
+            w_up, (0, start + peer // g * BLOCK, peer % g * cw), (held, BLOCK, cw)
+        )
+
+    coming = []
+    for d in sorted(range(1, n), key=lambda d: abs(2 * d - n)):
+        moved = lax.ppermute(piece((me + d) % n), "expert", [(e, (e + d) % n) for e in range(n)])
+        coming.append(((me + n - d) % n, moved))
+    coming.append((me, piece(me)))
+
+    first = merge_blocks(slab.reshape(experts, BLOCK, cw), order, anchor_of, cluster_ids, weight, n, g)
+    first, ready = serve(first, n, m, g, half, width, 1)
+
+    slab = jnp.zeros((n, held, BLOCK, cw), w_up.dtype)
+    for source, moved in coming:
+        slab = lax.dynamic_update_slice(slab, moved[None], (source + ready[0, 0], 0, 0, 0))
+    second = merge_blocks(slab.reshape(experts, BLOCK, cw), order, anchor_of, cluster_ids, weight, n, g)
+    second, _ = serve(second, n, m, g, half, width, 2)
+    outs = [part.reshape(m, half, width // m) for part in (first, second)]
+    return jnp.concatenate(outs, axis=1).reshape(1, m * units, width // m)
 
 
 def solution(mesh):

time: 473 us -> 529 us (1.12)
  Pallas kernels: 426 us -> 310 us
  waiting for transfers between devices: 25.5 us -> 103 us
  starting transfers between devices: 0.42 us -> 61.1 us
  local copies, waits for them, and re-layouts: 3.56 us -> 22.8 us
  between operations: 0.24 us -> 6.67 us
    pallas_call x1, Pallas kernels: 274 us -> 139 us  [deal(): pl.pallas_call(functools.partial(deal_kernel, n, g), out_shape=[jax.Shape...]
    ppermute x2 -> x19, waiting for transfers between devices: 25.5 us -> 103 us  [the longest x6 59.4 us: merge_blocks(): other = lax.ppermute(polar, 'expert', pairs(d))]
    ppermute x2 -> x19, starting transfers between devices: 0.42 us -> 61.1 us  [the longest x7 53.4 us: on_device(): lax.ppermute(piece((me + d) % n), 'expert', [(e, (e + d) % n) for e in ra...]
    pallas_call x1 -> x2, Pallas kernels: 22.4 us -> 40 us  [block_gram(): pl.pallas_call(gram_kernel, grid_spec=pltpu.PrefetchScalarGridSpec(num_sc...]
    pallas_call x1 -> x2, Pallas kernels: 23.2 us -> 40.2 us  [merge_rows(): pl.pallas_call(merge_kernel, grid_spec=pltpu.PrefetchScalarGridSpec(num_s...]
    pallas_call x1 -> x2, Pallas kernels: 106 us -> 91.1 us  [serve(): pl.pallas_call(functools.partial(serve_kernel, n, m, g, units), out_shape...]
    dynamic_slice x1 -> x3, local copies, waits for them, and re-layouts: 0.06 us -> 10.2 us  [the longest x1 9.28 us: piece(): lax.dynamic_slice(w_up, (0, start + peer // g * BLOCK, peer % g * cw), (h...]
    dynamic_update_slice x1 -> x14, local copies, waits for them, and re-layouts: 0.05 us -> 7.85 us  [the longest x8 7.68 us: on_device(): lax.dynamic_update_slice(slab, moved[None], (source + ready[0, 0], 0, 0, 0))]
  transfers between devices with their start and end apart: 2 -> 19, of which waited for: 2 -> 9; matrix products, arithmetic and copies ran while one was open for 0% -> 5% of each run, Pallas kernels for 0% -> 12%
where the time goes in v2:
time: 529 us; the launch traced here: 525 us
  Pallas kernels  310 us (59%)
  waiting for transfers between devices  103 us (19%)
  starting transfers between devices  61.1 us (12%)
  local copies, waits for them, and re-layouts  22.8 us (4%)
  matrix products  14 us (3%)
  other arithmetic  6.95 us (1%)
  between operations  6.67 us (1%)
    pallas_call x1, Pallas kernels, deal(): pl.pallas_call(functools.partial(deal_kernel, n, g), out_shape=[jax.Shape...  139 us
    pallas_call x2, Pallas kernels, serve(): pl.pallas_call(functools.partial(serve_kernel, n, m, g, units), out_shape...  91.1 us
    ppermute x6, waiting for transfers between devices, merge_blocks(): other = lax.ppermute(polar, 'expert', pairs(d))  59.4 us
    ppermute x7, starting transfers between devices, on_device(): lax.ppermute(piece((me + d) % n), 'expert', [(e, (e + d) % n) for e in ra...  53.4 us
    pallas_call x2, Pallas kernels, merge_rows(): pl.pallas_call(merge_kernel, grid_spec=pltpu.PrefetchScalarGridSpec(num_s...  40.2 us
    pallas_call x2, Pallas kernels, block_gram(): pl.pallas_call(gram_kernel, grid_spec=pltpu.PrefetchScalarGridSpec(num_sc...  40 us
    ppermute x7, waiting for transfers between devices, on_device(): lax.ppermute(piece((me + d) % n), 'expert', [(e, (e + d) % n) for e in ra...  23.5 us
    ppermute x6, waiting for transfers between devices, merge_blocks(): gram = gram + lax.ppermute(other, 'expert', pairs(d))  20.3 us
  transfers between devices with their start and end apart: 19, of which 9 were waited for; matrix products, arithmetic and copies ran while one was open for 5% of the time, Pallas kernels for 12%

profile of v2, /device:TPU:17, one launch (start us, length us, event | category | flops | bytes accessed | tf_op | source)
XLA Modules:
  0.0 525.0 jit_solution(1645837668134113015)
XLA Ops:
  0.0 0.7 subtract_add_fusion
  0.7 0.9 convert_reduce_fusion
  1.6 0.8 select_reduce_fusion.2
  2.4 1.4 select_reduce_fusion.1
  3.9 139.1 %deal.1 = (bf16[8,4,96,1024]{3,2,1,0:T(8,128)(2,1)}, s32[8,128]{1,0:T(8,128)S(1)}) custom-call(bf16[4,384,4096]{2,1,0:T(8,128)(2,1)} %w_ref.1), custom_call_target="tpu_custom_call" | custom-call | bytes 25165824 | tf_op jit(solution)/shard_map/deal/pallas_call | solution.py:63
  142.9 20.0 %gram.2 = f32[32,96,96]{2,1,0:T(8,128)S(1)} custom-call(s32[32]{0:T(128)S(1)} %select_reduce_fusion.order_ref, s32[32]{0:T(128)S(1)} %get-tuple-element.15.anchor_ref, bf16[32,96,1024]{2,1,0:T(8,128)(2,1)} %bitcast.93, bf16[32,96,1024]{2,1,0:T(8,128)(2,1)} %bitcast.94), custom_call_target="tpu_custom_call" | custom-call | flops 603979776 | bytes 12582912 | tf_op jit(solution)/shard_map/gram/pallas_call | solution.py:92
  162.9 0.8 constant_dynamic-slice_fusion.12
  163.8 2.4 collective-permute-start.2
  166.1 0.5 slice.4
  167.6 9.3 %constant_dynamic-slice_fusion.3 = (bf16[4,96,1024]{2,1,0:T(8,128)(2,1)}, bf16[4,96,1024]{2,1,0:T(8,128)(2,1)}, bf16[4,96,1024]{2,1,0:T(8,128)(2,1)}, bf16[4,96,...) fusion(bf16[4,384,4096]{2,1,0:T(8,128)(2,1)} %w_ref.1, ...), kind=kLoop, calls=%fused_computation.63 | loop fusion | bytes 11010104 | tf_op jit(solution)/shard_map/dynamic_slice | solution.py:320
  176.9 1.1 collective-permute-start.6
  178.0 1.2 collective-permute-start.7
  179.2 0.6 convert_element_type.21
  179.9 2.1 collective-permute-start.8
  182.0 2.3 collective-permute-done.2
  184.5 0.6 fusion.14
  185.2 0.4 multiply_subtract_fusion.3
  185.6 0.5 fusion.20
  186.5 0.5 fusion.21
  187.0 0.4 fusion.11
  187.4 0.5 fusion.22
  188.2 0.5 fusion.23
  189.1 0.5 fusion.24
  190.0 0.5 fusion.25
  190.9 0.5 fusion.26
  191.5 0.4 constant_dynamic-update-slice_fusion.6
  191.9 0.4 collective-permute-start.4
  192.3 45.1 %collective-permute-done.3 = bf16[8,96,96]{2,1,0:T(8,128)(2,1)S(1)} collective-permute-done((bf16[8,96,96]{2,1,0:T(8,128)(2,1)S(1)}, bf16[8,96,96]{2,1,0:T(8,128)(2,1)S(1)}, u32[]{:S(2)}, u32[]{:S(2)}) %collective-permute-start.3) | collective-permute-done | bytes 147488 | tf_op jit(solution)/shard_map/ppermute | solution.py:287
  237.6 4.9 collective-permute-done.5
  242.5 42.8 %collective-permute-start.10 = (bf16[4,96,1024]{2,1,0:T(8,128)(2,1)}, bf16[4,96,1024]{2,1,0:T(8,128)(2,1)}, u32[]{:S(2)}, u32[]{:S(2)}) collective-permute-start(bf16[4,96,1024]{2,1,0:T(8,128)(2,1)} %get-tuple-element.23), channel_id=1, source_target_pairs={{0,24},{4,28},{8,0},{12,4},{16,8},{20,12},{24,16},{28,20},{1,25},{... | collective-permute-start | bytes 2359304 | tf_op jit(solution)/shard_map/ppermute | solution.py:326
  285.3 20.1 %merge.2.merged_ref = bf16[8,96,1024]{2,1,0:T(8,128)(2,1)S(1)} custom-call(s32[32]{0:T(128)S(1)} %select_reduce_fusion.order_ref, s32[32]{0:T(128)S(1)} %bitcast.88, f32[32]{0:T(128)S(1)} %convert_divide_fusion.weight_ref, bf16[32,96,96]{2,1,0:T(8,128)(2,1)S(1)} %constant_dynamic-update-slice_fusion.3.factor_ref, bf16[32,96,1024]{2,1,0:T(8,128)(2,1)} %bitcast.95), custom_call_target="tpu_custom_call" | custom-call | flops 603979776 | bytes 9437184 | tf_op jit(solution)/shard_map/merge/pallas_call | solution.py:133
  305.4 42.6 %serve.2 = (bf16[1,768,1024]{2,1,0:T(8,128)(2,1)S(1)}, s32[8,128]{1,0:T(8,128)S(1)}) custom-call(bf16[8,96,1024]{2,1,0:T(8,128)(2,1)S(1)} %merge.2.merged_ref), custom_call_target="tpu_custom_call" | custom-call | bytes 3145728 | tf_op jit(solution)/shard_map/serve/pallas_call | solution.py:249
  348.0 0.5 slice.5
  353.7 0.8 broadcast_in_dim.99
  354.5 1.2 bitcast_dynamic-update-slice_fusion.7
  355.8 6.1 %collective-permute-start.12 = (bf16[4,96,1024]{2,1,0:T(8,128)(2,1)S(1)}, bf16[4,96,1024]{2,1,0:T(8,128)(2,1)S(1)}, u32[]{:S(2)}, u32[]{:S(2)}) collective-permute-start(bf16[4,96,1024]{2,1,0:T(8,128)(2,1)S(1)} %copy-done.2), channel_id=1, source_target_pairs={{0,28},{4,0},{8,4},{12,8},{16,12},{20,16},{24,20},{28,24},{1,29},{... | collective-permute-start | bytes 2359304 | tf_op jit(solution)/shard_map/ppermute | solution.py:326
  361.8 1.2 bitcast_dynamic-update-slice_fusion.6
  363.0 1.2 bitcast_dynamic-update-slice_fusion.5
  364.2 1.2 bitcast_dynamic-update-slice_fusion.4
  365.5 1.2 bitcast_dynamic-update-slice_fusion.3
  366.7 20.3 %collective-permute-done.11 = bf16[4,96,1024]{2,1,0:T(8,128)(2,1)S(1)} collective-permute-done((bf16[4,96,1024]{2,1,0:T(8,128)(2,1)}, bf16[4,96,1024]{2,1,0:T(8,128)(2,1)S(1)}, u32[]{:S(2)}, u32[]{:S(2)}) %collective-permute-start.11) | collective-permute-done | bytes 786464 | tf_op jit(solution)/shard_map/ppermute | solution.py:326
  387.0 3.2 collective-permute-done.12
  390.3 1.6 bitcast_dynamic-update-slice_fusion
  391.9 2.7 copy-done.1
  394.6 20.0 %gram.3 = f32[32,96,96]{2,1,0:T(8,128)S(1)} custom-call(s32[32]{0:T(128)S(1)} %select_reduce_fusion.order_ref, s32[32]{0:T(128)S(1)} %get-tuple-element.15.anchor_ref, bf16[32,96,1024]{2,1,0:T(8,128)(2,1)} %bitcast.90, bf16[32,96,1024]{2,1,0:T(8,128)(2,1)} %bitcast.91), custom_call_target="tpu_custom_call" | custom-call | flops 603979776 | bytes 12582912 | tf_op jit(solution)/shard_map/gram/pallas_call | solution.py:92
  414.8 2.3 collective-permute-start.15
  417.1 6.9 %collective-permute-done.13 = f32[8,96,96]{2,1,0:T(8,128)S(1)} collective-permute-done((f32[8,96,96]{2,1,0:T(8,128)S(1)}, f32[8,96,96]{2,1,0:T(8,128)S(1)}, u32[]{:S(2)}, u32[]{:S(2)}) %collective-permute-start.13) | collective-permute-done | bytes 294944 | tf_op jit(solution)/shard_map/ppermute | solution.py:282
  423.9 11.1 %collective-permute-done.15 = f32[8,96,96]{2,1,0:T(8,128)S(1)} collective-permute-done((f32[8,96,96]{2,1,0:T(8,128)S(1)}, f32[8,96,96]{2,1,0:T(8,128)S(1)}, u32[]{:S(2)}, u32[]{:S(2)}) %collective-permute-start.15) | collective-permute-done | bytes 294944 | tf_op jit(solution)/shard_map/ppermute | solution.py:282
  435.3 0.6 fusion.15
  435.9 0.4 multiply_subtract_fusion.1
  436.4 0.5 fusion.27
  437.2 0.5 fusion.28
  438.1 0.5 fusion.29
  438.9 0.5 fusion.30
  439.8 0.5 fusion.31
  440.6 0.5 fusion.32
  441.5 0.5 fusion.33
  442.1 0.4 constant_dynamic-update-slice_fusion.1
  442.6 2.3 collective-permute-start.18
  444.9 4.5 collective-permute-done.16
  449.5 5.0 collective-permute-done.18
  454.5 20.1 %merge.3.merged_ref = bf16[8,96,1024]{2,1,0:T(8,128)(2,1)S(1)} custom-call(s32[32]{0:T(128)S(1)} %select_reduce_fusion.order_ref, s32[32]{0:T(128)S(1)} %bitcast.89, f32[32]{0:T(128)S(1)} %convert_divide_fusion.weight_ref, bf16[32,96,96]{2,1,0:T(8,128)(2,1)S(1)} %constant_dynamic-update-slice_fusion.2.factor_ref, bf16[32,96,1024]{2,1,0:T(8,128)(2,1)} %bitcast.92), custom_call_target="tpu_custom_call" | custom-call | flops 603979776 | bytes 9437184 | tf_op jit(solution)/shard_map/merge/pallas_call | solution.py:133
  474.6 48.5 %serve.3 = (bf16[1,768,1024]{2,1,0:T(8,128)(2,1)S(1)}, s32[8,128]{1,0:T(8,128)}) custom-call(bf16[8,96,1024]{2,1,0:T(8,128)(2,1)S(1)} %merge.3.merged_ref), custom_call_target="tpu_custom_call" | custom-call | bytes 3145728 | tf_op jit(solution)/shard_map/serve/pallas_call | solution.py:249
  523.0 2.0 pad_maximum_fusion
  (57 shorter events, 5.5 us)
Async XLA Ops:
  163.8 16.1 %copy-start = (s32[32,1]{0,1:T(1,128)S(1)}, s32[32,1]{0,1:T(1,128)}, u32[]{:S(2)}) copy-start(s32[32,1]{0,1:T(1,128)} %param.4) | copy-start | bytes 388
  163.8 16.1 %collective-permute-start = (f32[8,96,96]{2,1,0:T(8,128)}, f32[8,96,96]{2,1,0:T(8,128)S(1)}, u32[]{:S(2)}, u32[]{:S(2)}) collective-permute-start(f32[8,96,96]{2,1,0:T(8,128)} %get-tuple-element.31), channel_id=1, source_target_pairs={{0,4},{4,8},{8,12},{12,0},{16,20},{20,24},{24,28},{28,16},{1,5},{5... | collective-permute-start | bytes 884744 | tf_op jit(solution)/shard_map/ppermute | solution.py:282
  163.8 18.3 %collective-permute-start.1 = (f32[8,96,96]{2,1,0:T(8,128)S(1)}, f32[8,96,96]{2,1,0:T(8,128)S(1)}, u32[]{:S(2)}, u32[]{:S(2)}) collective-permute-start(f32[8,96,96]{2,1,0:T(8,128)S(1)} %get-tuple-element.33), channel_id=1, source_target_pairs={{0,8},{4,12},{8,0},{12,4},{16,24},{20,28},{24,16},{28,20},{1,9},{5... | collective-permute-start | bytes 884744 | tf_op jit(solution)/shard_map/ppermute | solution.py:282
  163.8 20.6 %collective-permute-start.2 = (f32[8,96,96]{2,1,0:T(8,128)S(1)}, f32[8,96,96]{2,1,0:T(8,128)S(1)}, u32[]{:S(2)}, u32[]{:S(2)}) collective-permute-start(f32[8,96,96]{2,1,0:T(8,128)S(1)} %get-tuple-element.32), channel_id=1, source_target_pairs={{0,12},{4,0},{8,4},{12,8},{16,28},{20,16},{24,20},{28,24},{1,13},{... | collective-permute-start | bytes 884744 | tf_op jit(solution)/shard_map/ppermute | solution.py:282
  176.9 176.8 %collective-permute-start.6 = (bf16[4,96,1024]{2,1,0:T(8,128)(2,1)}, bf16[4,96,1024]{2,1,0:T(8,128)(2,1)}, u32[]{:S(2)}, u32[]{:S(2)}) collective-permute-start(bf16[4,96,1024]{2,1,0:T(8,128)(2,1)} %get-tuple-element.27), channel_id=1, source_target_pairs={{0,16},{4,20},{8,24},{12,28},{16,0},{20,4},{24,8},{28,12},{1,17},{... | collective-permute-start | bytes 2359304 | tf_op jit(solution)/shard_map/ppermute | solution.py:326
  178.0 177.7 %collective-permute-start.7 = (bf16[4,96,1024]{2,1,0:T(8,128)(2,1)}, bf16[4,96,1024]{2,1,0:T(8,128)(2,1)}, u32[]{:S(2)}, u32[]{:S(2)}) collective-permute-start(bf16[4,96,1024]{2,1,0:T(8,128)(2,1)} %get-tuple-element.26), channel_id=1, source_target_pairs={{0,12},{4,16},{8,20},{12,24},{16,28},{20,0},{24,4},{28,8},{1,13},{... | collective-permute-start | bytes 2359304 | tf_op jit(solution)/shard_map/ppermute | solution.py:326
  179.9 183.1 %collective-permute-start.8 = (bf16[4,96,1024]{2,1,0:T(8,128)(2,1)}, bf16[4,96,1024]{2,1,0:T(8,128)(2,1)}, u32[]{:S(2)}, u32[]{:S(2)}) collective-permute-start(bf16[4,96,1024]{2,1,0:T(8,128)(2,1)} %get-tuple-element.25), channel_id=1, source_target_pairs={{0,20},{4,24},{8,28},{12,0},{16,4},{20,8},{24,12},{28,16},{1,21},{... | collective-permute-start | bytes 2359304 | tf_op jit(solution)/shard_map/ppermute | solution.py:326
  187.4 5.0 copy-start.3
  191.9 45.5 %collective-permute-start.3 = (bf16[8,96,96]{2,1,0:T(8,128)(2,1)S(1)}, bf16[8,96,96]{2,1,0:T(8,128)(2,1)S(1)}, u32[]{:S(2)}, u32[]{:S(2)}) collective-permute-start(bf16[8,96,96]{2,1,0:T(8,128)(2,1)S(1)} %get-tuple-element.35), channel_id=1, source_target_pairs={{0,4},{4,8},{8,12},{12,0},{16,20},{20,24},{24,28},{28,16},{1,5},{5... | collective-permute-start | bytes 442376 | tf_op jit(solution)/shard_map/ppermute | solution.py:287
  191.9 45.5 %collective-permute-start.4 = (bf16[8,96,96]{2,1,0:T(8,128)(2,1)S(1)}, bf16[8,96,96]{2,1,0:T(8,128)(2,1)S(1)}, u32[]{:S(2)}, u32[]{:S(2)}) collective-permute-start(bf16[8,96,96]{2,1,0:T(8,128)(2,1)S(1)} %get-tuple-element.35), channel_id=1, source_target_pairs={{0,8},{4,12},{8,0},{12,4},{16,24},{20,28},{24,16},{28,20},{1,9},{5... | collective-permute-start | bytes 442376 | tf_op jit(solution)/shard_map/ppermute | solution.py:287
  237.4 5.1 collective-permute-start.5
  237.4 126.8 %collective-permute-start.9 = (bf16[4,96,1024]{2,1,0:T(8,128)(2,1)}, bf16[4,96,1024]{2,1,0:T(8,128)(2,1)}, u32[]{:S(2)}, u32[]{:S(2)}) collective-permute-start(bf16[4,96,1024]{2,1,0:T(8,128)(2,1)} %get-tuple-element.24), channel_id=1, source_target_pairs={{0,8},{4,12},{8,16},{12,20},{16,24},{20,28},{24,0},{28,4},{1,9},{5... | collective-permute-start | bytes 2359304 | tf_op jit(solution)/shard_map/ppermute | solution.py:326
  242.5 123.0 %collective-permute-start.10 = (bf16[4,96,1024]{2,1,0:T(8,128)(2,1)}, bf16[4,96,1024]{2,1,0:T(8,128)(2,1)}, u32[]{:S(2)}, u32[]{:S(2)}) collective-permute-start(bf16[4,96,1024]{2,1,0:T(8,128)(2,1)} %get-tuple-element.23), channel_id=1, source_target_pairs={{0,24},{4,28},{8,0},{12,4},{16,8},{20,12},{24,16},{28,20},{1,25},{... | collective-permute-start | bytes 2359304 | tf_op jit(solution)/shard_map/ppermute | solution.py:326
  305.4 50.4 %copy-start.2 = (bf16[4,96,1024]{2,1,0:T(8,128)(2,1)S(1)}, bf16[4,96,1024]{2,1,0:T(8,128)(2,1)}, u32[]{:S(2)}) copy-start(bf16[4,96,1024]{2,1,0:T(8,128)(2,1)} %get-tuple-element.21) | copy-start | bytes 2359300
  353.7 33.3 %collective-permute-start.11 = (bf16[4,96,1024]{2,1,0:T(8,128)(2,1)}, bf16[4,96,1024]{2,1,0:T(8,128)(2,1)S(1)}, u32[]{:S(2)}, u32[]{:S(2)}) collective-permute-start(bf16[4,96,1024]{2,1,0:T(8,128)(2,1)} %get-tuple-element.22), channel_id=1, source_target_pairs={{0,4},{4,8},{8,12},{12,16},{16,20},{20,24},{24,28},{28,0},{1,5},{5... | collective-permute-start | bytes 2359304 | tf_op jit(solution)/shard_map/ppermute | solution.py:326
  355.8 34.5 %collective-permute-start.12 = (bf16[4,96,1024]{2,1,0:T(8,128)(2,1)S(1)}, bf16[4,96,1024]{2,1,0:T(8,128)(2,1)S(1)}, u32[]{:S(2)}, u32[]{:S(2)}) collective-permute-start(bf16[4,96,1024]{2,1,0:T(8,128)(2,1)S(1)} %copy-done.2), channel_id=1, source_target_pairs={{0,28},{4,0},{8,4},{12,8},{16,12},{20,16},{24,20},{28,24},{1,29},{... | collective-permute-start | bytes 2359304 | tf_op jit(solution)/shard_map/ppermute | solution.py:326
  391.9 2.7 copy-start.1
  414.7 9.3 %collective-permute-start.13 = (f32[8,96,96]{2,1,0:T(8,128)S(1)}, f32[8,96,96]{2,1,0:T(8,128)S(1)}, u32[]{:S(2)}, u32[]{:S(2)}) collective-permute-start(f32[8,96,96]{2,1,0:T(8,128)S(1)} %get-tuple-element.28), channel_id=1, source_target_pairs={{0,4},{4,8},{8,12},{12,0},{16,20},{20,24},{24,28},{28,16},{1,5},{5... | collective-permute-start | bytes 884744 | tf_op jit(solution)/shard_map/ppermute | solution.py:282
  414.7 9.2 %collective-permute-start.14 = (f32[8,96,96]{2,1,0:T(8,128)S(1)}, f32[8,96,96]{2,1,0:T(8,128)S(1)}, u32[]{:S(2)}, u32[]{:S(2)}) collective-permute-start(f32[8,96,96]{2,1,0:T(8,128)S(1)} %get-tuple-element.30), channel_id=1, source_target_pairs={{0,8},{4,12},{8,0},{12,4},{16,24},{20,28},{24,16},{28,20},{1,9},{5... | collective-permute-start | bytes 884744 | tf_op jit(solution)/shard_map/ppermute | solution.py:282
  414.8 20.3 %collective-permute-start.15 = (f32[8,96,96]{2,1,0:T(8,128)S(1)}, f32[8,96,96]{2,1,0:T(8,128)S(1)}, u32[]{:S(2)}, u32[]{:S(2)}) collective-permute-start(f32[8,96,96]{2,1,0:T(8,128)S(1)} %get-tuple-element.29), channel_id=1, source_target_pairs={{0,12},{4,0},{8,4},{12,8},{16,28},{20,16},{24,20},{28,24},{1,13},{... | collective-permute-start | bytes 884744 | tf_op jit(solution)/shard_map/ppermute | solution.py:282
  442.5 6.9 %collective-permute-start.16 = (bf16[8,96,96]{2,1,0:T(8,128)(2,1)S(1)}, bf16[8,96,96]{2,1,0:T(8,128)(2,1)S(1)}, u32[]{:S(2)}, u32[]{:S(2)}) collective-permute-start(bf16[8,96,96]{2,1,0:T(8,128)(2,1)S(1)} %get-tuple-element.37), channel_id=1, source_target_pairs={{0,4},{4,8},{8,12},{12,0},{16,20},{20,24},{24,28},{28,16},{1,5},{5... | collective-permute-start | bytes 442376 | tf_op jit(solution)/shard_map/ppermute | solution.py:287
  442.5 6.9 %collective-permute-start.17 = (bf16[8,96,96]{2,1,0:T(8,128)(2,1)S(1)}, bf16[8,96,96]{2,1,0:T(8,128)(2,1)S(1)}, u32[]{:S(2)}, u32[]{:S(2)}) collective-permute-start(bf16[8,96,96]{2,1,0:T(8,128)(2,1)S(1)} %get-tuple-element.37), channel_id=1, source_target_pairs={{0,8},{4,12},{8,0},{12,4},{16,24},{20,28},{24,16},{28,20},{1,9},{5... | collective-permute-start | bytes 442376 | tf_op jit(solution)/shard_map/ppermute | solution.py:287
  442.6 11.8 %collective-permute-start.18 = (bf16[8,96,96]{2,1,0:T(8,128)(2,1)S(1)}, bf16[8,96,96]{2,1,0:T(8,128)(2,1)S(1)}, u32[]{:S(2)}, u32[]{:S(2)}) collective-permute-start(bf16[8,96,96]{2,1,0:T(8,128)(2,1)S(1)} %get-tuple-element.37), channel_id=1, source_target_pairs={{0,12},{4,0},{8,4},{12,8},{16,28},{20,16},{24,20},{28,24},{1,13},{... | collective-permute-start | bytes 442376 | tf_op jit(solution)/shard_map/ppermute | solution.py:287

commit v3 on v1

--- a/solution.py
+++ b/solution.py
@@ -77,67 +77,61 @@
     )(w)
 
 
-def gram_kernel(order_ref, anchor_ref, lead_ref, rows_ref, gram_ref):
-    gram_ref[0] = lax.dot_general(
-        lead_ref[0], rows_ref[0], (((1,), (1,)), ((), ())), preferred_element_type=jnp.float32
-    )
+def gram_kernel(order_ref, anchor_ref, slab_ref, gram_ref):
+    def one(place, carry):
+        expert = order_ref[place]
+        gram_ref[place] = lax.dot_general(
+            slab_ref[anchor_ref[expert]],
+            slab_ref[expert],
+            (((1,), (1,)), ((), ())),
+            preferred_element_type=jnp.float32,
+        )
+        return carry
+
+    lax.fori_loop(0, gram_ref.shape[0], one, 0, unroll=4)
 
 
 def block_gram(order, anchor_of, slab):
-    experts, _, cw = slab.shape
+    places = order.shape[0]
+    _, _, cw = slab.shape
+    scalars = pl.BlockSpec(memory_space=pltpu.SMEM)
     return pl.pallas_call(
         gram_kernel,
-        grid_spec=pltpu.PrefetchScalarGridSpec(
-            num_scalar_prefetch=2,
-            grid=(experts,),
-            in_specs=[
-                pl.BlockSpec((1, BLOCK, cw), lambda s, order, anchor: (anchor[order[s]], 0, 0)),
-                pl.BlockSpec((1, BLOCK, cw), lambda s, order, anchor: (order[s], 0, 0)),
-            ],
-            out_specs=pl.BlockSpec((1, BLOCK, BLOCK), lambda s, order, anchor: (order[s], 0, 0)),
-        ),
-        out_shape=jax.ShapeDtypeStruct((experts, BLOCK, BLOCK), jnp.float32),
+        in_specs=[scalars, scalars, pl.BlockSpec(memory_space=pltpu.VMEM)],
+        out_specs=pl.BlockSpec(memory_space=pltpu.VMEM),
+        out_shape=jax.ShapeDtypeStruct((places, BLOCK, BLOCK), jnp.float32),
         compiler_params=pltpu.CompilerParams(vmem_limit_bytes=VMEM_BYTES),
         cost_estimate=pl.CostEstimate(
-            flops=2 * slab.size * BLOCK, bytes_accessed=4 * slab.size, transcendentals=0
+            flops=2 * places * BLOCK * BLOCK * cw, bytes_accessed=2 * slab.size, transcendentals=0
         ),
         name="gram",
-    )(order, anchor_of, slab, slab)
-
-
-def merge_kernel(order_ref, cluster_ref, weight_ref, factor_ref, rows_ref, merged_ref, total_ref):
-    step = pl.program_id(0)
-    expert = order_ref[step]
-    last = order_ref[jnp.maximum(step - 1, 0)]
-    opens = (step == 0) | (cluster_ref[last] != cluster_ref[expert])
-    turned = jnp.dot(factor_ref[0], rows_ref[0], preferred_element_type=jnp.float32)
-    aligned = (turned * weight_ref[expert]).astype(jnp.bfloat16).astype(jnp.float32)
-
-    @pl.when(opens)
-    def _():
-        total_ref[...] = aligned
-
-    @pl.when(jnp.logical_not(opens))
-    def _():
-        total_ref[...] += aligned
-
-    merged_ref[0] = total_ref[...].astype(merged_ref.dtype)
+    )(order, anchor_of, slab)
+
+
+def merge_kernel(order_ref, cluster_ref, weight_ref, factor_ref, slab_ref, merged_ref, total_ref):
+    def one(place, last):
+        expert = order_ref[place]
+        here = cluster_ref[expert]
+        turned = jnp.dot(factor_ref[place], slab_ref[expert], preferred_element_type=jnp.float32)
+        aligned = (turned * weight_ref[expert]).astype(jnp.bfloat16).astype(jnp.float32)
+        total = jnp.where(here == last, total_ref[...], 0.0) + aligned
+        total_ref[...] = total
+        merged_ref[here] = total.astype(merged_ref.dtype)
+        return here
+
+    total_ref[...] = jnp.zeros_like(total_ref)
+    lax.fori_loop(0, factor_ref.shape[0], one, jnp.int32(-1), unroll=2)
 
 
 def merge_rows(order, cluster_ids, weight, factors, slab, clusters):
     experts, _, cw = slab.shape
+    scalars = pl.BlockSpec(memory_space=pltpu.SMEM)
+    whole = pl.BlockSpec(memory_space=pltpu.VMEM)
     return pl.pallas_call(
         merge_kernel,
-        grid_spec=pltpu.PrefetchScalarGridSpec(
-            num_scalar_prefetch=3,
-            grid=(experts,),
-            in_specs=[
-                pl.BlockSpec((1, BLOCK, BLOCK), lambda s, order, ids, weight: (order[s], 0, 0)),
-                pl.BlockSpec((1, BLOCK, cw), lambda s, order, ids, weight: (order[s], 0, 0)),
-            ],
-            out_specs=pl.BlockSpec((1, BLOCK, cw), lambda s, order, ids, weight: (ids[order[s]], 0, 0)),
-            scratch_shapes=[pltpu.VMEM((BLOCK, cw), jnp.float32)],
-        ),
+        in_specs=[scalars, scalars, scalars, whole, whole],
+        out_specs=whole,
+        scratch_shapes=[pltpu.VMEM((BLOCK, cw), jnp.float32)],
         out_shape=jax.ShapeDtypeStruct((clusters, BLOCK, cw), slab.dtype),
         compiler_params=pltpu.CompilerParams(vmem_limit_bytes=VMEM_BYTES),
         cost_estimate=pl.CostEstimate(
@@ -282,7 +276,6 @@
     )
     place = jnp.sum(before.astype(jnp.int32), axis=1)
     order = jnp.sum(jnp.where(place[None, :] == index[:, None], index[None, :], 0), axis=1)
-    partial = block_gram(order, anchor_of, slab)
 
     share = experts // g
     part = lax.axis_index("expert") % g
@@ -290,10 +283,13 @@
     def pairs(d):
         return [(e, e // g * g + (e + d) % g) for e in range(n)]
 
-    gram = lax.dynamic_slice_in_dim(partial, part * share, share)
-    for d in range(1, g):
-        other = lax.dynamic_slice_in_dim(partial, (part + d) % g * share, share)
-        gram = gram + lax.ppermute(other, "expert", pairs(d))
+    def share_gram(d):
+        return block_gram(lax.dynamic_slice_in_dim(order, (part + d) % g * share, share), anchor_of, slab)
+
+    arriving = [lax.ppermute(share_gram(d), "expert", pairs(d)) for d in range(1, g)]
+    gram = share_gram(0)
+    for other in arriving:
+        gram = gram + other
     polar = newton_schulz(gram).astype(jnp.bfloat16)
     factors = jnp.zeros((experts, BLOCK, BLOCK), jnp.bfloat16)
     factors = lax.dynamic_update_slice_in_dim(factors, polar, part * share, 0)

time: 473 us -> 444 us (0.939)
  Pallas kernels: 426 us -> 405 us
  waiting for transfers between devices: 25.5 us -> 18.7 us
    pallas_call x2 -> x3, Pallas kernels: 45.5 us -> 24.7 us  [the longest x2 13.7 us: block_gram(): pl.pallas_call(gram_kernel, in_specs=[scalars, scalars, pl.BlockSpec(memo...]
    ppermute x1, waiting for transfers between devices: 17.6 us -> 10.7 us  [on_device(): lax.ppermute(share_gram(d), 'expert', pairs(d))]
  transfers between devices with their start and end apart: 2 -> 2, of which waited for: 2 -> 2; matrix products, arithmetic and copies ran while one was open for 0% -> 0% of each run, Pallas kernels for 0% -> 2%
where the time goes in v3:
time: 444 us
  Pallas kernels  405 us (91%)
  waiting for transfers between devices  18.7 us (4%)
  matrix products  12 us (3%)
    pallas_call x1, Pallas kernels, deal(): pl.pallas_call(functools.partial(deal_kernel, n, g), out_shape=jax.ShapeD...  274 us
    pallas_call x1, Pallas kernels, serve(): pl.pallas_call(functools.partial(serve_kernel, n, m, g, units), out_shape...  106 us
    pallas_call x2, Pallas kernels, block_gram(): pl.pallas_call(gram_kernel, in_specs=[scalars, scalars, pl.BlockSpec(memo...  13.7 us
    pallas_call x1, Pallas kernels, merge_rows(): pl.pallas_call(merge_kernel, in_specs=[scalars, scalars, scalars, whole,...  11 us
    ppermute x1, waiting for transfers between devices, on_device(): lax.ppermute(share_gram(d), 'expert', pairs(d))  10.7 us
  transfers between devices with their start and end apart: 2, of which 2 were waited for; matrix products, arithmetic and copies ran while one was open for 0% of the time, Pallas kernels for 2%

profile of v3, /device:TPU:17, one launch (start us, length us, event | category | flops | bytes accessed | tf_op | source)
XLA Modules:
  0.0 443.5 jit_solution(3085374344022563217)
XLA Ops:
  0.0 0.9 convert_reduce_fusion
  0.9 0.1 select_reduce_fusion.order_ref
  1.0 0.7 subtract_add_fusion
  1.7 0.8 select_reduce_fusion.2
  2.5 0.9 select_reduce_fusion.1
  3.3 273.9 %deal.1 = bf16[8,4,96,2048]{3,2,1,0:T(8,128)(2,1)} custom-call(bf16[4,384,4096]{2,1,0:T(8,128)(2,1)} %w_ref.1), custom_call_target="tpu_custom_call" | custom-call | bytes 25165824 | tf_op jit(solution)/shard_map/deal/pallas_call | solution.py:62
  277.2 0.1 fusion.12
  277.3 6.8 %gram.3 = f32[16,96,96]{2,1,0:T(8,128)S(1)} custom-call(s32[16]{0:T(128)S(1)} %get-tuple-element.9.order_ref, s32[32]{0:T(128)S(1)} %get-tuple-element.5.anchor_ref, bf16[32,96,2048]{2,1,0:T(8,128)(2,1)} %bitcast.36), custom_call_target="tpu_custom_call" | custom-call | flops 603979776 | bytes 12582912 | tf_op jit(solution)/shard_map/gram/pallas_call | solution.py:98
  284.2 0.1 collective-permute-start
  284.3 6.8 %gram.2 = f32[16,96,96]{2,1,0:T(8,128)S(1)} custom-call(s32[16]{0:T(128)S(1)} %get-tuple-element.10.order_ref, s32[32]{0:T(128)S(1)} %get-tuple-element.5.anchor_ref, bf16[32,96,2048]{2,1,0:T(8,128)(2,1)} %bitcast.37), custom_call_target="tpu_custom_call" | custom-call | flops 603979776 | bytes 12582912 | tf_op jit(solution)/shard_map/gram/pallas_call | solution.py:98
  291.1 10.7 %collective-permute-done = f32[16,96,96]{2,1,0:T(8,128)S(1)} collective-permute-done((f32[16,96,96]{2,1,0:T(8,128)S(1)}, f32[16,96,96]{2,1,0:T(8,128)S(1)}, u32[]{:S(2)}, u32[]{:S(2)}) %collective-permute-start) | collective-permute-done | bytes 589856 | tf_op jit(solution)/shard_map/ppermute | solution.py:289
  301.9 0.3 multiply_reduce_fusion
  302.1 1.0 fusion.7
  303.2 0.6 multiply_subtract_fusion.1
  303.8 0.9 fusion.13
  304.7 0.5 multiply_subtract_fusion
  305.3 0.9 fusion.14
  306.2 0.5 fusion.5
  306.8 0.9 fusion.15
  307.7 0.5 fusion.4
  308.2 0.9 fusion.16
  309.2 0.5 fusion.3
  309.7 0.9 fusion.17
  310.6 0.5 fusion.2
  311.2 0.9 fusion.18
  312.1 0.6 fusion.1
  312.7 0.0 copy-start.1
  312.7 0.0 copy-start.2
  312.7 0.9 fusion.19
  313.6 0.1 broadcast_in_dim.71
  313.8 0.7 constant_dynamic-update-slice_fusion
  314.4 0.4 collective-permute-start.1
  314.8 0.0 copy-done.1
  314.8 0.1 select_reduce_fusion.3
  314.9 0.0 copy-done.2
  314.9 7.9 %collective-permute-done.1 = bf16[16,96,96]{2,1,0:T(8,128)(2,1)S(1)} collective-permute-done((bf16[16,96,96]{2,1,0:T(8,128)(2,1)S(1)}, bf16[16,96,96]{2,1,0:T(8,128)(2,1)S(1)}, u32[]{:S(2)}, u32[]{:S(2)}) %collective-permute-start.1) | collective-permute-done | bytes 294944 | tf_op jit(solution)/shard_map/ppermute | solution.py:297
  322.8 0.1 constant_dynamic-update-slice_fusion.1.factor_ref
  322.9 11.0 %merge.1.merged_ref = bf16[8,96,2048]{2,1,0:T(8,128)(2,1)S(1)} custom-call(s32[32]{0:T(128)S(1)} %select_reduce_fusion.order_ref, s32[32]{0:T(128)S(1)} %bitcast.35, f32[32]{0:T(128)S(1)} %convert_divide_fusion.weight_ref, bf16[32,96,96]{2,1,0:T(8,128)(2,1)S(1)} %constant_dynamic-update-slice_fusion.1.factor_ref, bf16[32,96,2048]{2,1,0:T(8,128)(2,1)} %bitcast.38), custom_call_target="tpu_custom_call" | custom-call | flops 1207959552 | bytes 18874368 | tf_op jit(solution)/shard_map/merge/pallas_call | solution.py:130
  333.9 0.0 copy-start
  333.9 1.7 copy-done
  335.6 106.3 %serve.1 = bf16[1,1536,1024]{2,1,0:T(8,128)(2,1)S(1)} custom-call(bf16[8,96,2048]{2,1,0:T(8,128)(2,1)} %copy-done), custom_call_target="tpu_custom_call" | custom-call | bytes 6291456 | tf_op jit(solution)/shard_map/serve/pallas_call | solution.py:238
  441.9 1.7 copy.7
  (4 shorter events, 0.0 us)
Async XLA Ops:
  284.2 17.7 %collective-permute-start = (f32[16,96,96]{2,1,0:T(8,128)S(1)}, f32[16,96,96]{2,1,0:T(8,128)S(1)}, u32[]{:S(2)}, u32[]{:S(2)}) collective-permute-start(f32[16,96,96]{2,1,0:T(8,128)S(1)} %gram.3), channel_id=1, source_target_pairs={{0,4},{4,0},{8,12},{12,8},{16,20},{20,16},{24,28},{28,24},{1,5},{5... | collective-permute-start | bytes 1769480 | tf_op jit(solution)/shard_map/ppermute | solution.py:289
  312.7 2.1 copy-start.1
  312.7 2.2 copy-start.2
  314.4 8.4 %collective-permute-start.1 = (bf16[16,96,96]{2,1,0:T(8,128)(2,1)S(1)}, bf16[16,96,96]{2,1,0:T(8,128)(2,1)S(1)}, u32[]{:S(2)}, u32[]{:S(2)}) collective-permute-start(bf16[16,96,96]{2,1,0:T(8,128)(2,1)S(1)} %get-tuple-element.12), channel_id=1, source_target_pairs={{0,4},{4,0},{8,12},{12,8},{16,20},{20,16},{24,28},{28,24},{1,5},{5... | collective-permute-start | bytes 884744 | tf_op jit(solution)/shard_map/ppermute | solution.py:297
  333.9 1.7 copy-start

commit v4 on v3

--- a/solution.py
+++ b/solution.py
@@ -9,6 +9,7 @@
 
 BLOCK = 96
 NS_STEPS = 8
+PAIR = 2
 MESH = pl.DeviceIdType.MESH
 VMEM_BYTES = 48 * 1024 * 1024
 
@@ -24,49 +25,84 @@
     return value
 
 
-def deal_kernel(n, g, w_ref, slab_ref, local_sem, send_sem, recv_sem):
+def deal_kernel(n, gp, w_ref, slab_ref, local_sem, send_sem, recv_sem):
     me, unit = lax.axis_index("expert"), lax.axis_index("unit")
     cw = slab_ref.shape[-1]
+    half = n // PAIR
+    side = lax.rem(unit, PAIR)
+    feeder = unit - side + me // half
+    own = me // half == side
     barrier = pltpu.get_barrier_semaphore()
-    for d in range(1, n):
-        pl.semaphore_signal(barrier, inc=1, device_id=(lax.rem(me + d, n), unit), device_id_type=MESH)
-    pl.semaphore_wait(barrier, n - 1)
-
-    def piece(peer):
-        rows = pl.ds(pl.multiple_of((peer // g) * BLOCK, BLOCK), BLOCK)
-        columns = pl.ds(pl.multiple_of(lax.rem(peer, g) * cw, cw), cw)
+    for d in range(n):
+        source = lax.rem(me + d, n)
+
+        @pl.when((d != 0) | jnp.logical_not(own))
+        def _():
+            pl.semaphore_signal(barrier, inc=1, device_id=(source, feeder), device_id_type=MESH)
+    pl.semaphore_wait(barrier, n - own.astype(jnp.int32))
+
+    def piece(place, to):
+        rows = pl.ds(pl.multiple_of(place // gp * BLOCK, BLOCK), BLOCK)
+        columns = pl.ds(pl.multiple_of((lax.rem(place, gp) * PAIR + to) * cw, cw), cw)
         return w_ref.at[:, rows, columns]
 
-    copies = []
-    for d in sorted(range(1, n), key=lambda d: abs(2 * d - n)):
-        peer = lax.rem(me + d, n)
-        copy = pltpu.make_async_remote_copy(
-            src_ref=piece(peer),
+    def remote(i, to):
+        place = lax.rem(me + i, half)
+        return pltpu.make_async_remote_copy(
+            src_ref=piece(place, to),
             dst_ref=slab_ref.at[me],
-            send_sem=send_sem.at[d],
-            recv_sem=recv_sem.at[d],
-            device_id=(peer, unit),
+            send_sem=send_sem.at[i, to],
+            recv_sem=recv_sem.at[me],
+            device_id=(side * half + place, unit - side + to),
             device_id_type=MESH,
         )
-        copy.start()
-        copies.append(copy)
-    own = pltpu.make_async_copy(piece(me), slab_ref.at[me], local_sem)
-    own.start()
-    own.wait()
-    for copy in copies:
-        copy.wait()
-
-
-def deal(w, n, g):
+
+    def local():
+        return pltpu.make_async_copy(piece(lax.rem(me, half), side), slab_ref.at[me], local_sem)
+
+    for i in sorted(range(half), key=lambda i: abs(2 * i - half)):
+        for to in range(PAIR):
+            @pl.when((i != 0) | (to != side) | jnp.logical_not(own))
+            def _():
+                remote(i, to).start()
+
+    @pl.when(own)
+    def _():
+        local().start()
+        local().wait()
+
+    for i in range(half):
+        for to in range(PAIR):
+            @pl.when((i != 0) | (to != side) | jnp.logical_not(own))
+            def _():
+                remote(i, to).wait_send()
+
+    for d in range(n):
+        source = lax.rem(me + d, n)
+
+        @pl.when((d != 0) | jnp.logical_not(own))
+        def _():
+            landed = slab_ref.at[source]
+            pltpu.make_async_remote_copy(
+                src_ref=landed,
+                dst_ref=landed,
+                send_sem=send_sem.at[0, 0],
+                recv_sem=recv_sem.at[source],
+                device_id=(source, feeder),
+                device_id_type=MESH,
+            ).wait_recv()
+
+
+def deal(w, n, g, gp):
     held, units, width = w.shape
     return pl.pallas_call(
-        functools.partial(deal_kernel, n, g),
+        functools.partial(deal_kernel, n, gp),
         out_shape=jax.ShapeDtypeStruct((n, held, BLOCK, width // g), w.dtype),
         in_specs=[pl.BlockSpec(memory_space=pl.ANY)],
         out_specs=pl.BlockSpec(memory_space=pl.ANY),
         scratch_shapes=[
             pltpu.SemaphoreType.DMA,
-            pltpu.SemaphoreType.DMA((n,)),
+            pltpu.SemaphoreType.DMA((n // PAIR, PAIR)),
             pltpu.SemaphoreType.DMA((n,)),
         ],
         compiler_params=pltpu.CompilerParams(
@@ -141,31 +177,34 @@
     )(order, cluster_ids, weight, factors, slab)
 
 
-def serve_kernel(n, m, g, units, merged_ref, out_ref, local_sem, send_sem, recv_sem):
+def serve_kernel(n, m, gp, units, merged_ref, out_ref, local_sem, send_sem, recv_sem):
     me, unit = lax.axis_index("expert"), lax.axis_index("unit")
     cw, uw = merged_ref.shape[-1], out_ref.shape[-1]
     pw = min(cw, uw)
     parts = cw // pw
 
+    def first_column(source, u):
+        return (lax.rem(source, gp) * PAIR + lax.rem(u, PAIR)) * cw
+
     def target(part):
-        column = lax.rem(me, g) * cw + part * pw
+        column = first_column(me, unit) + part * pw
         return column // uw, pl.multiple_of(lax.rem(column, uw), pw)
 
-    def feeds(source):
-        column = lax.rem(source, g) * cw
+    def feeds(source, u):
+        column = first_column(source, u)
         return (column // uw <= unit) & (unit <= (column + cw - pw) // uw)
 
     barrier = pltpu.get_barrier_semaphore()
     for d in range(n):
         source = lax.rem(me + n - d, n)
         for u in range(m):
-            @pl.when(feeds(source) & ((u != unit) | (d != 0)))
+            @pl.when(feeds(source, u) & ((u != unit) | (d != 0)))
             def _():
                 pl.semaphore_signal(barrier, inc=1, device_id=(source, u), device_id_type=MESH)
-    own = feeds(me)
+    own = feeds(me, unit)
     pl.semaphore_wait(barrier, n * parts - own.astype(jnp.int32))
 
-    rows = pl.ds(pl.multiple_of(unit * units + (me // g) * BLOCK, BLOCK), BLOCK)
+    rows = pl.ds(pl.multiple_of((unit - lax.rem(unit, PAIR)) * units + me // gp * BLOCK, BLOCK), BLOCK)
 
     def remote(d, part):
         peer = lax.rem(me + d, n)
@@ -218,10 +257,10 @@
     for d in range(n):
         source = lax.rem(me + n - d, n)
         for u in range(m):
-            @pl.when(feeds(source) & ((u != unit) | (d != 0)))
+            @pl.when(feeds(source, u) & ((u != unit) | (d != 0)))
             def _():
-                there = pl.ds(pl.multiple_of(u * units + (source // g) * BLOCK, BLOCK), BLOCK)
-                column = pl.multiple_of(lax.rem(lax.rem(source, g) * cw, uw), pw)
+                there = pl.ds(pl.multiple_of((u - u % PAIR) * units + source // gp * BLOCK, BLOCK), BLOCK)
+                column = pl.multiple_of(lax.rem(first_column(source, u), uw), pw)
                 landed = out_ref.at[0, there, pl.ds(column, pw)]
                 pltpu.make_async_remote_copy(
                     src_ref=landed,
@@ -233,10 +272,10 @@
                 ).wait_recv()
 
 
-def serve(merged, n, m, g, units, width):
+def serve(merged, n, m, gp, units, width):
     parts = max(1, merged.shape[-1] * m // width)
     return pl.pallas_call(
-        functools.partial(serve_kernel, n, m, g, units),
+        functools.partial(serve_kernel, n, m, gp, units),
         out_shape=jax.ShapeDtypeStruct((1, m * units, width // m), merged.dtype),
         in_specs=[pl.BlockSpec(memory_space=pl.ANY)],
         out_specs=pl.BlockSpec(memory_space=pl.ANY),
@@ -256,8 +295,8 @@
 def on_device(w_up, cluster, counts):
     n, m = lax.axis_size("expert"), lax.axis_size("unit")
     held, units, width = w_up.shape
-    nblocks = units // BLOCK
-    g = n // nblocks
+    gp = n // (PAIR * units // BLOCK)
+    g = gp * PAIR
     cluster_ids = cluster[:, 0]
     experts = cluster_ids.shape[0]
     index = jnp.arange(experts, dtype=jnp.int32)
@@ -270,7 +309,7 @@
     total = jnp.sum(jnp.where(member, counts[None, :], 0), axis=1).astype(jnp.float32)
     weight = counts.astype(jnp.float32) / jnp.sum(jnp.where(member, total[:, None], 0.0), axis=0)
 
-    slab = deal(w_up, n, g).reshape(experts, BLOCK, width // g)
+    slab = deal(w_up, n, g, gp).reshape(experts, BLOCK, width // g)
     before = (cluster_ids[None, :] < cluster_ids[:, None]) | (
         (cluster_ids[None, :] == cluster_ids[:, None]) & (index[None, :] < index[:, None])
     )
@@ -278,15 +317,20 @@
     order = jnp.sum(jnp.where(place[None, :] == index[:, None], index[None, :], 0), axis=1)
 
     share = experts // g
-    part = lax.axis_index("expert") % g
+    part = lax.axis_index("expert") % gp * PAIR + lax.axis_index("unit") % PAIR
 
     def pairs(d):
-        return [(e, e // g * g + (e + d) % g) for e in range(n)]
+        moves = []
+        for e in range(n):
+            for u in range(m):
+                to = (e % gp * PAIR + u % PAIR + d) % g
+                moves.append((e * m + u, (e // gp * gp + to // PAIR) * m + u // PAIR * PAIR + to % PAIR))
+        return moves
 
     def share_gram(d):
         return block_gram(lax.dynamic_slice_in_dim(order, (part + d) % g * share, share), anchor_of, slab)
 
-    arriving = [lax.ppermute(share_gram(d), "expert", pairs(d)) for d in range(1, g)]
+    arriving = [lax.ppermute(share_gram(d), ("expert", "unit"), pairs(d)) for d in range(1, g)]
     gram = share_gram(0)
     for other in arriving:
         gram = gram + other
@@ -294,11 +338,11 @@
     factors = jnp.zeros((experts, BLOCK, BLOCK), jnp.bfloat16)
     factors = lax.dynamic_update_slice_in_dim(factors, polar, part * share, 0)
     for d in range(1, g):
-        other = lax.ppermute(polar, "expert", pairs(d))
+        other = lax.ppermute(polar, ("expert", "unit"), pairs(d))
         factors = lax.dynamic_update_slice_in_dim(factors, other, (part + g - d) % g * share, 0)
 
     merged = merge_rows(order, cluster_ids, weight, factors, slab, n)
-    return serve(merged, n, m, g, units, width)
+    return serve(merged, n, m, gp, units, width)
 
 
 def solution(mesh):

time: 444 us -> 395 us (0.89)
  Pallas kernels: 405 us -> 308 us
  starting transfers between devices: 0.42 us -> 65.8 us
  waiting for transfers between devices: 18.7 us -> 1.6 us
    pallas_call x2, Pallas kernels: 380 us -> 283 us  [the longest x1 208 us: deal(): pl.pallas_call(functools.partial(deal_kernel, n, gp), out_shape=jax.Shape...]
    ppermute x2, starting transfers between devices: 0.42 us -> 65.8 us  [the longest x1 65.7 us: on_device(): lax.ppermute(share_gram(d), ('expert', 'unit'), pairs(d))]
    ppermute x2, waiting for transfers between devices: 18.7 us -> 1.6 us  [the longest x1 1.59 us: on_device(): other = lax.ppermute(polar, ('expert', 'unit'), pairs(d))]
  transfers between devices with their start and end apart: 2 -> 2, of which waited for: 2 -> 1; matrix products, arithmetic and copies ran while one was open for 0% -> 0% of each run, Pallas kernels for 2% -> 2%
where the time goes in v4:
time: 395 us
  Pallas kernels  308 us (78%)
  starting transfers between devices  65.8 us (17%)
  matrix products  12 us (3%)
    pallas_call x1, Pallas kernels, deal(): pl.pallas_call(functools.partial(deal_kernel, n, gp), out_shape=jax.Shape...  208 us
    pallas_call x1, Pallas kernels, serve(): pl.pallas_call(functools.partial(serve_kernel, n, m, gp, units), out_shap...  75.4 us
    ppermute x1, starting transfers between devices, on_device(): lax.ppermute(share_gram(d), ('expert', 'unit'), pairs(d))  65.7 us
    pallas_call x2, Pallas kernels, block_gram(): pl.pallas_call(gram_kernel, in_specs=[scalars, scalars, pl.BlockSpec(memo...  13.7 us
    pallas_call x1, Pallas kernels, merge_rows(): pl.pallas_call(merge_kernel, in_specs=[scalars, scalars, scalars, whole,...  11 us
  transfers between devices with their start and end apart: 2, of which 1 were waited for; matrix products, arithmetic and copies ran while one was open for 0% of the time, Pallas kernels for 2%

profile of v4, /device:TPU:17, one launch (start us, length us, event | category | flops | bytes accessed | tf_op | source)
XLA Modules:
  0.0 394.8 jit_solution(5434039745346704580)
XLA Ops:
  0.0 0.9 convert_reduce_fusion
  0.9 0.1 select_reduce_fusion.order_ref
  1.0 0.7 subtract_add_fusion
  1.7 0.8 select_reduce_fusion.2
  2.5 0.9 select_reduce_fusion.1
  3.3 207.7 %deal.1 = bf16[8,4,96,2048]{3,2,1,0:T(8,128)(2,1)} custom-call(bf16[4,384,4096]{2,1,0:T(8,128)(2,1)} %w_ref.1), custom_call_target="tpu_custom_call" | custom-call | bytes 25165824 | tf_op jit(solution)/shard_map/deal/pallas_call | solution.py:98
  211.1 0.1 fusion.12
  211.1 6.8 %gram.3 = f32[16,96,96]{2,1,0:T(8,128)S(1)} custom-call(s32[16]{0:T(128)S(1)} %get-tuple-element.9.order_ref, s32[32]{0:T(128)S(1)} %get-tuple-element.5.anchor_ref, bf16[32,96,2048]{2,1,0:T(8,128)(2,1)} %bitcast.36), custom_call_target="tpu_custom_call" | custom-call | flops 603979776 | bytes 12582912 | tf_op jit(solution)/shard_map/gram/pallas_call | solution.py:134
  218.0 65.7 %collective-permute-start = (f32[16,96,96]{2,1,0:T(8,128)S(1)}, f32[16,96,96]{2,1,0:T(8,128)S(1)}, u32[]{:S(2)}, u32[]{:S(2)}) collective-permute-start(f32[16,96,96]{2,1,0:T(8,128)S(1)} %gram.3), channel_id=1, source_target_pairs={{0,1},{1,0},{2,3},{3,2},{4,5},{5,4},{6,7},{7,6},{8,9},{9,8},{10,11... | collective-permute-start | bytes 1769480 | tf_op jit(solution)/shard_map/ppermute | solution.py:333
  283.7 6.8 %gram.2 = f32[16,96,96]{2,1,0:T(8,128)S(1)} custom-call(s32[16]{0:T(128)S(1)} %get-tuple-element.10.order_ref, s32[32]{0:T(128)S(1)} %get-tuple-element.5.anchor_ref, bf16[32,96,2048]{2,1,0:T(8,128)(2,1)} %bitcast.37), custom_call_target="tpu_custom_call" | custom-call | flops 603979776 | bytes 12582912 | tf_op jit(solution)/shard_map/gram/pallas_call | solution.py:134
  290.6 0.0 collective-permute-done
  290.6 0.3 multiply_reduce_fusion
  290.9 1.0 fusion.7
  291.9 0.6 multiply_subtract_fusion.1
  292.5 0.9 fusion.13
  293.5 0.5 multiply_subtract_fusion
  294.0 0.9 fusion.14
  295.0 0.5 fusion.5
  295.5 0.9 fusion.15
  296.4 0.5 fusion.4
  297.0 0.9 fusion.16
  297.9 0.5 fusion.3
  298.4 0.9 fusion.17
  299.4 0.5 fusion.2
  299.9 0.9 fusion.18
  300.8 0.6 fusion.1
  301.4 0.0 copy-start.1
  301.4 0.0 copy-start.2
  301.4 0.9 fusion.19
  302.4 0.1 broadcast_in_dim.71
  302.5 0.7 constant_dynamic-update-slice_fusion
  303.2 0.1 collective-permute-start.1
  303.3 0.0 copy-done.1
  303.3 0.1 select_reduce_fusion.3
  303.4 0.0 copy-done.2
  303.4 1.6 collective-permute-done.1
  305.0 0.1 constant_dynamic-update-slice_fusion.1.factor_ref
  305.0 11.0 %merge.1.merged_ref = bf16[8,96,2048]{2,1,0:T(8,128)(2,1)S(1)} custom-call(s32[32]{0:T(128)S(1)} %select_reduce_fusion.order_ref, s32[32]{0:T(128)S(1)} %bitcast.35, f32[32]{0:T(128)S(1)} %convert_divide_fusion.weight_ref, bf16[32,96,96]{2,1,0:T(8,128)(2,1)S(1)} %constant_dynamic-update-slice_fusion.1.factor_ref, bf16[32,96,2048]{2,1,0:T(8,128)(2,1)} %bitcast.38), custom_call_target="tpu_custom_call" | custom-call | flops 1207959552 | bytes 18874368 | tf_op jit(solution)/shard_map/merge/pallas_call | solution.py:166
  316.0 0.0 copy-start
  316.0 1.7 copy-done
  317.7 75.4 %serve.1 = bf16[1,1536,1024]{2,1,0:T(8,128)(2,1)S(1)} custom-call(bf16[8,96,2048]{2,1,0:T(8,128)(2,1)} %copy-done), custom_call_target="tpu_custom_call" | custom-call | bytes 6291456 | tf_op jit(solution)/shard_map/serve/pallas_call | solution.py:277
  393.1 1.7 copy.7
  (4 shorter events, 0.0 us)
Async XLA Ops:
  218.0 72.6 %collective-permute-start = (f32[16,96,96]{2,1,0:T(8,128)S(1)}, f32[16,96,96]{2,1,0:T(8,128)S(1)}, u32[]{:S(2)}, u32[]{:S(2)}) collective-permute-start(f32[16,96,96]{2,1,0:T(8,128)S(1)} %gram.3), channel_id=1, source_target_pairs={{0,1},{1,0},{2,3},{3,2},{4,5},{5,4},{6,7},{7,6},{8,9},{9,8},{10,11... | collective-permute-start | bytes 1769480 | tf_op jit(solution)/shard_map/ppermute | solution.py:333
  301.4 1.9 copy-start.1
  301.4 1.9 copy-start.2
  303.2 1.8 collective-permute-start.1
  316.0 1.7 copy-start

commit v5 on v4

--- a/solution.py
+++ b/solution.py
@@ -277,7 +277,7 @@
     return pl.pallas_call(
         functools.partial(serve_kernel, n, m, gp, units),
         out_shape=jax.ShapeDtypeStruct((1, m * units, width // m), merged.dtype),
-        in_specs=[pl.BlockSpec(memory_space=pl.ANY)],
+        in_specs=[pl.BlockSpec(memory_space=pltpu.VMEM)],
         out_specs=pl.BlockSpec(memory_space=pl.ANY),
         scratch_shapes=[
             pltpu.SemaphoreType.DMA,

time: 395 us -> 397 us (level)
  no operation moved by 1% of the time
where the time goes in v5:
time: 397 us; the launch traced here: 396 us
  Pallas kernels  309 us (78%)
  starting transfers between devices  65.8 us (17%)
  matrix products  12 us (3%)
    pallas_call x1, Pallas kernels, deal(): pl.pallas_call(functools.partial(deal_kernel, n, gp), out_shape=jax.Shape...  208 us
    pallas_call x1, Pallas kernels, serve(): pl.pallas_call(functools.partial(serve_kernel, n, m, gp, units), out_shap...  77.1 us
    ppermute x1, starting transfers between devices, on_device(): lax.ppermute(share_gram(d), ('expert', 'unit'), pairs(d))  65.7 us
    pallas_call x2, Pallas kernels, block_gram(): pl.pallas_call(gram_kernel, in_specs=[scalars, scalars, pl.BlockSpec(memo...  13.7 us
    pallas_call x1, Pallas kernels, merge_rows(): pl.pallas_call(merge_kernel, in_specs=[scalars, scalars, scalars, whole,...  11 us
  transfers between devices with their start and end apart: 2, of which 1 were waited for; matrix products, arithmetic and copies ran while one was open for 0% of the time, Pallas kernels for 2%

profile of v5, /device:TPU:17, one launch (start us, length us, event | category | flops | bytes accessed | tf_op | source)
XLA Modules:
  0.0 396.5 jit_solution(4236289012651169905)
XLA Ops:
  0.0 0.9 convert_reduce_fusion
  0.9 0.1 select_reduce_fusion.order_ref
  1.0 0.7 subtract_add_fusion
  1.7 0.8 select_reduce_fusion.2
  2.5 0.9 select_reduce_fusion.1
  3.3 207.7 %deal.1 = bf16[8,4,96,2048]{3,2,1,0:T(8,128)(2,1)} custom-call(bf16[4,384,4096]{2,1,0:T(8,128)(2,1)} %w_ref.1), custom_call_target="tpu_custom_call" | custom-call | bytes 25165824 | tf_op jit(solution)/shard_map/deal/pallas_call | solution.py:98
  211.1 0.1 fusion.12
  211.1 6.8 %gram.3 = f32[16,96,96]{2,1,0:T(8,128)S(1)} custom-call(s32[16]{0:T(128)S(1)} %get-tuple-element.9.order_ref, s32[32]{0:T(128)S(1)} %get-tuple-element.5.anchor_ref, bf16[32,96,2048]{2,1,0:T(8,128)(2,1)} %bitcast.36), custom_call_target="tpu_custom_call" | custom-call | flops 603979776 | bytes 12582912 | tf_op jit(solution)/shard_map/gram/pallas_call | solution.py:134
  218.0 65.7 %collective-permute-start = (f32[16,96,96]{2,1,0:T(8,128)S(1)}, f32[16,96,96]{2,1,0:T(8,128)S(1)}, u32[]{:S(2)}, u32[]{:S(2)}) collective-permute-start(f32[16,96,96]{2,1,0:T(8,128)S(1)} %gram.3), channel_id=1, source_target_pairs={{0,1},{1,0},{2,3},{3,2},{4,5},{5,4},{6,7},{7,6},{8,9},{9,8},{10,11... | collective-permute-start | bytes 1769480 | tf_op jit(solution)/shard_map/ppermute | solution.py:333
  283.7 6.8 %gram.2 = f32[16,96,96]{2,1,0:T(8,128)S(1)} custom-call(s32[16]{0:T(128)S(1)} %get-tuple-element.10.order_ref, s32[32]{0:T(128)S(1)} %get-tuple-element.5.anchor_ref, bf16[32,96,2048]{2,1,0:T(8,128)(2,1)} %bitcast.37), custom_call_target="tpu_custom_call" | custom-call | flops 603979776 | bytes 12582912 | tf_op jit(solution)/shard_map/gram/pallas_call | solution.py:134
  290.6 0.0 collective-permute-done
  290.6 0.3 multiply_reduce_fusion
  290.9 1.0 fusion.7
  291.9 0.6 multiply_subtract_fusion.1
  292.5 0.9 fusion.13
  293.5 0.5 multiply_subtract_fusion
  294.0 0.9 fusion.14
  295.0 0.5 fusion.5
  295.5 0.9 fusion.15
  296.4 0.5 fusion.4
  297.0 0.9 fusion.16
  297.9 0.5 fusion.3
  298.4 0.9 fusion.17
  299.4 0.5 fusion.2
  299.9 0.9 fusion.18
  300.8 0.6 fusion.1
  301.4 0.0 copy-start.1
  301.4 0.0 copy-start.2
  301.4 0.9 fusion.19
  302.4 0.1 broadcast_in_dim.71
  302.5 0.7 constant_dynamic-update-slice_fusion
  303.2 0.1 collective-permute-start.1
  303.3 0.0 copy-done.1
  303.3 0.1 select_reduce_fusion.3
  303.4 0.0 copy-done.2
  303.4 1.6 collective-permute-done.1
  305.0 0.1 constant_dynamic-update-slice_fusion.1.factor_ref
  305.0 11.0 %merge.1.merged_ref = bf16[8,96,2048]{2,1,0:T(8,128)(2,1)S(1)} custom-call(s32[32]{0:T(128)S(1)} %select_reduce_fusion.order_ref, s32[32]{0:T(128)S(1)} %bitcast.35, f32[32]{0:T(128)S(1)} %convert_divide_fusion.weight_ref, bf16[32,96,96]{2,1,0:T(8,128)(2,1)S(1)} %constant_dynamic-update-slice_fusion.1.factor_ref, bf16[32,96,2048]{2,1,0:T(8,128)(2,1)} %bitcast.38), custom_call_target="tpu_custom_call" | custom-call | flops 1207959552 | bytes 18874368 | tf_op jit(solution)/shard_map/merge/pallas_call | solution.py:166
  316.1 0.0 copy-start
  316.1 1.7 copy-done
  317.7 77.1 %serve.1 = bf16[1,1536,1024]{2,1,0:T(8,128)(2,1)S(1)} custom-call(bf16[8,96,2048]{2,1,0:T(8,128)(2,1)} %copy-done), custom_call_target="tpu_custom_call" | custom-call | bytes 6291456 | tf_op jit(solution)/shard_map/serve/pallas_call | solution.py:277
  394.8 1.7 copy.7
  (4 shorter events, 0.0 us)
Async XLA Ops:
  218.0 72.6 %collective-permute-start = (f32[16,96,96]{2,1,0:T(8,128)S(1)}, f32[16,96,96]{2,1,0:T(8,128)S(1)}, u32[]{:S(2)}, u32[]{:S(2)}) collective-permute-start(f32[16,96,96]{2,1,0:T(8,128)S(1)} %gram.3), channel_id=1, source_target_pairs={{0,1},{1,0},{2,3},{3,2},{4,5},{5,4},{6,7},{7,6},{8,9},{9,8},{10,11... | collective-permute-start | bytes 1769480 | tf_op jit(solution)/shard_map/ppermute | solution.py:333
  301.4 1.9 copy-start.1
  301.4 1.9 copy-start.2
  303.2 1.8 collective-permute-start.1
  316.1 1.7 copy-start
